TPU v7x, 32 devices: a whole 2x2x4 slice. The times are simulated.
32 devices in a mesh: row: 8 (over y, x, core), col: 4 (over z).
Axes of the slice: x: 2, y: 2, z: 4, core: 2. Of those that a mesh axis runs over, the one named last changes fastest.
Arguments:
- inputs: bfloat16 [256, 12288], P('col', 'row'), may hold values from -6 to 6
- w_up: bfloat16 [12288, 24576], P('row', 'col'), may hold values from -0.0546875 to 0.0546875
- w_down: bfloat16 [24576, 12288], P('col', 'row'), may hold values from -0.0390625 to 0.0390625
- mask_up: int32 [96, 192], P('row', 'col'), may hold values from 0 to 1, as said below
- mask_down: int32 [192, 96], P('col', 'row'), may hold values from 0 to 1, as said below
- cotangent: bfloat16 [256, 12288], P('col', 'row'), may hold values from -1.5 to 1.5
Outputs:
- outputs: bfloat16 [256, 12288], P('col', 'row')
- grad_inputs: bfloat16 [256, 12288], P('col', 'row')
- grad_up: bfloat16 [12288, 24576], P('row', 'col')
- grad_down: bfloat16 [24576, 12288], P('col', 'row')
Inputs may be any that keep to these rules, and one draw needn't show every extreme that they name: `mask_up`: each entry is 0 or 1; the chance of a 1 is the same along a row of tiles and differs from row to row, between 0.2 and 0.8. `mask_down`: each entry is 0 or 1; the chance of a 1 is the same along a row of tiles and differs from row to row, between 0.2 and 0.8.
All inputs are finite; a program needn't handle non-finite values.
Results may differ from a plain program's by a relative error of at most 0.029.
Values may be sent and summed in bfloat16 or wider, within the bound.
No kernel may reach another device: no remote copies, remote signals or barrier semaphores. Data moves between devices by JAX's collectives and lax.ppermute only.
A program may use at most 256 MiB of HBM per device.

v0:
```python
import jax
import jax.numpy as jnp
from jax import lax
from jax.sharding import PartitionSpec as P


def apply_mask(weight, mask):
    rows, cols = mask.shape
    tile = weight.shape[0] // rows
    shaped = weight.reshape(rows, tile, cols, tile)
    keep = mask[:, None, :, None].astype(weight.dtype)
    return (shaped * keep).reshape(weight.shape)


def smooth_gate(value):
    return jax.nn.gelu(value, approximate=True)


def activate(hidden, grad_act):
    act = smooth_gate(hidden).astype(jnp.bfloat16)
    _, pull = jax.vjp(smooth_gate, hidden)
    grad_hidden = pull(grad_act)[0].astype(jnp.bfloat16)
    return (act, grad_hidden)


def contract(left, right, left_dim, right_dim):
    return lax.dot_general(
        left, right, (((left_dim,), (right_dim,)), ((), ())), preferred_element_type=jnp.float32
    )


def per_device(inputs, w_up, w_down, mask_up, mask_down, cotangent):
    up_kept = apply_mask(w_up, mask_up)
    down_kept = apply_mask(w_down, mask_down)
    inputs_all, cot_all = (
        lax.all_gather(inputs, "col", axis=0, tiled=True),
        lax.all_gather(cotangent, "col", axis=0, tiled=True),
    )
    up_part = jnp.dot(inputs_all, up_kept, preferred_element_type=jnp.float32)
    back_part = contract(cot_all, down_kept, 1, 1)
    hidden, grad_act = (
        lax.psum_scatter(
            up_part.astype(jnp.bfloat16), "row", scatter_dimension=0, tiled=True
        ).astype(jnp.float32),
        lax.psum_scatter(
            back_part.astype(jnp.bfloat16), "row", scatter_dimension=0, tiled=True
        ).astype(jnp.float32),
    )
    act, grad_hidden = activate(hidden, grad_act)
    act_all, grad_all = (
        lax.all_gather(act, "row", axis=0, tiled=True),
        lax.all_gather(grad_hidden, "row", axis=0, tiled=True),
    )
    out_part = jnp.dot(act_all, down_kept, preferred_element_type=jnp.float32)
    input_part = contract(grad_all, up_kept, 1, 1)
    outputs, grad_inputs = (
        lax.psum_scatter(
            out_part.astype(jnp.bfloat16), "col", scatter_dimension=0, tiled=True
        ).astype(jnp.float32),
        lax.psum_scatter(
            input_part.astype(jnp.bfloat16), "col", scatter_dimension=0, tiled=True
        ).astype(jnp.float32),
    )
    grad_down = apply_mask(contract(act_all, cot_all, 0, 0).astype(jnp.bfloat16), mask_down)
    grad_up = apply_mask(contract(inputs_all, grad_all, 0, 0).astype(jnp.bfloat16), mask_up)
    return (outputs.astype(jnp.bfloat16), grad_inputs.astype(jnp.bfloat16), grad_up, grad_down)


def solution(mesh):
    in_specs = (
        P("col", "row"),
        P("row", "col"),
        P("col", "row"),
        P("row", "col"),
        P("col", "row"),
        P("col", "row"),
    )
    out_specs = (P("col", "row"), P("col", "row"), P("row", "col"), P("col", "row"))
    return jax.shard_map(
        per_device, mesh=mesh, in_specs=in_specs, out_specs=out_specs, check_vma=False
    )
```

profile of v0, /device:TPU:0, one launch (start us, length us, event | category | flops | bytes accessed | tf_op | source)
XLA Modules:
  0.0 377.9 jit_solution(16998974039851681638)
XLA Ops:
  7.2 21.8 %all_gather.14 = bf16[256,1536]{1,0:T(8,128)(2,1)} all-gather(bf16[64,1536]{1,0:T(8,128)(2,1)} %param.11), channel_id=1, replica_groups=mesh['row'=8,'col'=4] {'col'}, dimensions={0}, use_global_device_ids=true | all-gather | bytes 983040 | tf_op jit(solution)/shard_map/all_gather | solution.py:37
  29.0 24.6 %copy.25 = bf16[6144,1536]{0,1:T(8,128)(2,1)} copy(bf16[6144,1536]{1,0:T(8,128)(2,1)} %param.8) | data formatting | bytes 37748736 | tf_op args[2]
  53.6 6.9 %mul.90 = bf16[48,128,12,128]{1,0,3,2:T(8,128)(2,1)} broadcast(bf16[48,12]{0,1:T(8,128)(2,1)S(1)} %convert_element_type.58), dimensions={0,2} | broadcast | bytes 18875520 | tf_op jit(solution)/shard_map/mul | solution.py:12
  60.5 18.3 %fusion.4 = bf16[256,6144]{0,1:T(8,128)(2,1)S(1)} fusion(bf16[256,1536]{1,0:T(8,128)(2,1)} %all_gather.14, bf16[6144,1536]{0,1:T(8,128)(2,1)} %copy.25, bf16[192,8,48,128]{3,2,1,0:T(8,128)(2,1)} %bitcast.40), kind=kOutput, calls=%fused_computation.10 | convolution fusion | flops 4842848256 | bytes 41680896 | tf_op jit(solution)/shard_map/dot_general | solution.py:27
  78.8 3.1 copy.32
  82.0 18.4 %all_gather.12 = bf16[256,1536]{1,0:T(8,128)(2,1)} all-gather(bf16[64,1536]{1,0:T(8,128)(2,1)S(1)} %copy-done.2), channel_id=1, replica_groups=mesh['row'=8,'col'=4] {'col'}, dimensions={0}, use_global_device_ids=true | all-gather | bytes 983040 | tf_op jit(solution)/shard_map/all_gather | solution.py:36
  100.4 7.0 %mul.83 = bf16[12,128,48,128]{3,2,1,0:T(8,128)(2,1)} broadcast(bf16[12,48]{1,0:T(8,128)(2,1)S(1)} %convert_element_type.53), dimensions={0,2} | broadcast | bytes 18875520 | tf_op jit(solution)/shard_map/mul | solution.py:12
  107.4 18.6 %fusion.3 = bf16[256,6144]{0,1:T(8,128)(2,1)S(1)} fusion(bf16[256,1536]{1,0:T(8,128)(2,1)} %all_gather.12, bf16[1536,6144]{1,0:T(8,128)(2,1)} %param.7, bf16[192,8,48,128]{3,2,1,0:T(8,128)(2,1)} %bitcast.43), kind=kOutput, calls=%fused_computation.9 | convolution fusion | flops 4842848256 | bytes 41680896 | tf_op jit(solution)/shard_map/dot_general | solution.py:39
  126.0 3.1 copy.30
  129.2 48.9 %reduce-scatter.13.cloned.1.call-done = bf16[32,6144]{1,0:T(8,128)(2,1)} async-done(((bf16[256,6144]{1,0:T(8,128)(2,1)}), bf16[32,6144]{1,0:T(8,128)(2,1)}) %reduce-scatter.13.cloned.1.call-update) | async-done | bytes 393232 | tf_op jit(solution)/shard_map/reduce_scatter | solution.py:42
  178.1 2.6 fusion.14
  180.9 0.5 all-gather.5.cloned.1.call-update
  181.4 0.3 reduce-scatter.9.cloned.1.call-start
  181.7 20.6 %copy.49 = bf16[192,8,48,128]{3,1,2,0:T(8,128)(2,1)} copy(bf16[192,8,48,128]{3,2,1,0:T(8,128)(2,1)} %bitcast.44) | data formatting | bytes 37748736
  202.3 20.5 %copy.48 = bf16[192,8,48,128]{3,1,2,0:T(8,128)(2,1)} copy(bf16[192,8,48,128]{3,2,1,0:T(8,128)(2,1)} %bitcast.41) | data formatting | bytes 37748736
  222.8 24.8 %copy.27 = bf16[1536,6144]{0,1:T(8,128)(2,1)} copy(bf16[1536,6144]{1,0:T(8,128)(2,1)} %bitcast.47) | data formatting | bytes 37748736 | tf_op jit(solution)/shard_map/mul | solution.py:12
  247.6 24.7 %copy.28 = bf16[6144,1536]{1,0:T(8,128)(2,1)} copy(bf16[6144,1536]{0,1:T(8,128)(2,1)} %bitcast.46) | data formatting | bytes 37748736 | tf_op jit(solution)/shard_map/mul | solution.py:12
  272.3 18.3 %fusion.8 = bf16[256,1536]{1,0:T(8,128)(2,1)} fusion(bf16[256,6144]{1,0:T(8,128)(2,1)} %all-gather.3.cloned.1.call-done, bf16[6144,1536]{0,1:T(8,128)(2,1)} %copy.25, bf16[192,8,48,128]{3,2,1,0:T(8,128)(2,1)} %bitcast.42), kind=kOutput, calls=%fused_computation.15 | convolution fusion | flops 4841668608 | bytes 41680896 | tf_op jit(solution)/shard_map/dot_general | solution.py:54
  290.6 0.3 reduce-scatter.11.cloned.1.call-start
  291.0 18.6 %convolution_convert_fusion.4 = bf16[256,1536]{1,0:T(8,128)(2,1)} fusion(bf16[256,6144]{1,0:T(8,128)(2,1)} %all-gather.5.cloned.1.call-done, bf16[1536,6144]{1,0:T(8,128)(2,1)} %param.7, bf16[192,8,48,128]{3,2,1,0:T(8,128)(2,1)} %bitcast.45), kind=kOutput, calls=%fused_computation.14 | convolution fusion | flops 4841668608 | bytes 41680896 | tf_op jit(solution)/shard_map/dot_general | solution.py:27
  309.5 13.4 %fusion.2 = bf16[1536,6144]{0,1:T(8,128)(2,1)} fusion(bf16[1536,6144]{0,1:T(8,128)(2,1)} %copy.27, bf16[256,6144]{1,0:T(8,128)(2,1)S(1)} %copy-done.1, bf16[256,1536]{1,0:T(8,128)(2,1)} %all_gather.12), kind=kOutput, calls=%fused_computation.4 | convolution fusion | flops 4850712576 | bytes 41680896 | tf_op jit(solution)/shard_map/dot_general | solution.py:27
  322.9 24.7 %copy.29 = bf16[1536,6144]{1,0:T(8,128)(2,1)} copy(bf16[1536,6144]{0,1:T(8,128)(2,1)} %fusion.2) | data formatting | bytes 37748736
  347.7 13.5 %fusion = bf16[6144,1536]{1,0:T(8,128)(2,1)} fusion(bf16[6144,1536]{1,0:T(8,128)(2,1)} %copy.28, bf16[256,6144]{1,0:T(8,128)(2,1)S(1)} %copy-done, bf16[256,1536]{1,0:T(8,128)(2,1)} %all_gather.14), kind=kOutput, calls=%fused_computation.2 | convolution fusion | flops 4850712576 | bytes 41680896 | tf_op jit(solution)/shard_map/dot_general | solution.py:27
  361.2 9.9 %reduce-scatter.11.cloned.1.call-done = bf16[64,1536]{1,0:T(8,128)(2,1)} async-done(((bf16[256,1536]{1,0:T(8,128)(2,1)}), bf16[64,1536]{1,0:T(8,128)(2,1)}) %reduce-scatter.11.cloned.1.call-update) | async-done | bytes 196624 | tf_op jit(solution)/shard_map/reduce_scatter | solution.py:60
  (25 shorter events, 0.3 us)
Async XLA Ops:
  7.2 122.1 %reduce-scatter.15.cloned.1.call-start = ((), (), s32[]{:S(2)}) async-start(), calls=%async_computation.9 | async-start | bytes 3538944 | tf_op jit(solution)/shard_map/reduce_scatter | solution.py:45
  29.0 24.6 %copy-start.3 = (s32[48,12]{0,1:T(8,128)S(1)}, s32[48,12]{0,1:T(8,128)}, u32[]{:S(2)}) copy-start(s32[48,12]{0,1:T(8,128)} %param.10) | copy-start | bytes 6916
  60.5 21.5 %copy-start.4 = (s32[12,48]{1,0:T(8,128)S(1)}, s32[12,48]{1,0:T(8,128)}, u32[]{:S(2)}) copy-start(s32[12,48]{1,0:T(8,128)} %param.9) | copy-start | bytes 6916
  60.5 21.5 %copy-start.2 = (bf16[64,1536]{1,0:T(8,128)(2,1)S(1)}, bf16[64,1536]{1,0:T(8,128)(2,1)}, u32[]{:S(2)}) copy-start(bf16[64,1536]{1,0:T(8,128)(2,1)} %param.6) | copy-start | bytes 589828
  81.9 96.2 %reduce-scatter.13.cloned.1.call-start = ((), (), s32[]{:S(2)}) async-start(), calls=%async_computation.8 | async-start | bytes 3538944 | tf_op jit(solution)/shard_map/reduce_scatter | solution.py:42
  129.1 143.2 %all-gather.3.cloned.1.call-start = ((), (), s32[]{:S(2)}) async-start(), calls=%async_computation.4 | async-start | bytes 3538944 | tf_op jit(solution)/shard_map/all_gather | solution.py:51
  180.8 110.1 %all-gather.5.cloned.1.call-start = ((), (), s32[]{:S(2)}) async-start(), calls=%async_computation.6 | async-start | bytes 3538944 | tf_op jit(solution)/shard_map/all_gather | solution.py:52
  181.4 179.8 %reduce-scatter.9.cloned.1.call-start = ((), (), s32[]{:S(2)}) async-start(), calls=%async_computation.5 | async-start | bytes 983040 | tf_op jit(solution)/shard_map/reduce_scatter | solution.py:57
  290.6 80.5 %reduce-scatter.11.cloned.1.call-start = ((), (), s32[]{:S(2)}) async-start(), calls=%async_computation.7 | async-start | bytes 983040 | tf_op jit(solution)/shard_map/reduce_scatter | solution.py:60
  290.9 18.6 %copy-start.1 = (bf16[256,6144]{1,0:T(8,128)(2,1)S(1)}, bf16[256,6144]{1,0:T(8,128)(2,1)}, u32[]{:S(2)}) copy-start(bf16[256,6144]{1,0:T(8,128)(2,1)} %all-gather.5.cloned.1.call-done) | copy-start | bytes 9437188
  322.9 24.8 %copy-start = (bf16[256,6144]{1,0:T(8,128)(2,1)S(1)}, bf16[256,6144]{1,0:T(8,128)(2,1)}, u32[]{:S(2)}) copy-start(bf16[256,6144]{1,0:T(8,128)(2,1)} %all-gather.3.cloned.1.call-done) | copy-start | bytes 9437188
Sparse Core Ops, SparseCore 0:
  82.0 46.0 reduce-scatter.14
  131.9 46.2 reduce-scatter.12
  180.9 32.2 all-gather.2
  215.0 32.3 all-gather.4
  290.7 23.1 reduce-scatter.8
  347.8 23.2 reduce-scatter.10
where the time goes:
time: 381 us; the launch traced here: 378 us
  local copies, waits for them, and re-layouts  160 us (42%)
  matrix products  101 us (27%)
  waiting for transfers between devices  59.5 us (16%)
  blocking collectives  40.1 us (11%)
  between operations  14.2 us (4%)
    unnamed x16, local copies, waits for them, and re-layouts  96.7 us
    dot_general x4, matrix products, contract(): lax.dot_general(left, right, (((left_dim,), (right_dim,)), ((), ())), pre...  63.8 us
    mul x4, local copies, waits for them, and re-layouts, apply_mask(): return (shaped * keep).reshape(weight.shape)  63.4 us
    reduce_scatter x1, waiting for transfers between devices, per_device(): lax.psum_scatter(up_part.astype(jnp.bfloat16), 'row', scatter_dimension=0...  48.9 us
    all_gather x1, blocking collectives, per_device(): lax.all_gather(cotangent, 'col', axis=0, tiled=True)  21.8 us
    dot_general x1, matrix products, per_device(): up_part = jnp.dot(inputs_all, up_kept, preferred_element_type=jnp.float32)  18.6 us
    all_gather x1, blocking collectives, per_device(): lax.all_gather(inputs, 'col', axis=0, tiled=True)  18.4 us
    dot_general x1, matrix products, per_device(): out_part = jnp.dot(act_all, down_kept, preferred_element_type=jnp.float32)  18.3 us
  transfers between devices with their start and end apart: 6, of which 2 were waited for; matrix products, arithmetic and copies ran while one was open for 55% of the time, Pallas kernels for 0%

commit v1 on v0

v1 whole, which is shorter than its diff:
```python
import functools

import jax
import jax.numpy as jnp
from jax import lax
from jax.experimental import pallas as pl
from jax.experimental.pallas import tpu as pltpu
from jax.sharding import PartitionSpec as P

TILE = 128
MIB = 1 << 20
F32 = jnp.float32
BF16 = jnp.bfloat16


def smooth_gate(value):
    return jax.nn.gelu(value, approximate=True)


def contract(left, right, left_dim, right_dim):
    return lax.dot_general(
        left, right, (((left_dim,), (right_dim,)), ((), ())), preferred_element_type=F32
    )


def apply_mask(weight, mask):
    rows, cols = mask.shape
    tile = weight.shape[0] // rows
    shaped = weight.reshape(rows, tile, cols, tile)
    keep = mask[:, None, :, None].astype(weight.dtype)
    return (shaped * keep).reshape(weight.shape)


def activate(hidden, grad_act):
    act = smooth_gate(hidden).astype(BF16)
    _, pull = jax.vjp(smooth_gate, hidden)
    grad_hidden = pull(grad_act)[0].astype(BF16)
    return (act, grad_hidden)


def per_device_plain(inputs, w_up, w_down, mask_up, mask_down, cotangent):
    up_kept = apply_mask(w_up, mask_up)
    down_kept = apply_mask(w_down, mask_down)
    inputs_all, cot_all = (
        lax.all_gather(inputs, "col", axis=0, tiled=True),
        lax.all_gather(cotangent, "col", axis=0, tiled=True),
    )
    up_part = jnp.dot(inputs_all, up_kept, preferred_element_type=F32)
    back_part = contract(cot_all, down_kept, 1, 1)
    hidden, grad_act = (
        lax.psum_scatter(
            part.astype(BF16), "row", scatter_dimension=0, tiled=True
        ).astype(F32)
        for part in (up_part, back_part)
    )
    act, grad_hidden = activate(hidden, grad_act)
    act_all, grad_all = (
        lax.all_gather(act, "row", axis=0, tiled=True),
        lax.all_gather(grad_hidden, "row", axis=0, tiled=True),
    )
    out_part = jnp.dot(act_all, down_kept, preferred_element_type=F32)
    input_part = contract(grad_all, up_kept, 1, 1)
    outputs, grad_inputs = (
        lax.psum_scatter(
            part.astype(BF16), "col", scatter_dimension=0, tiled=True
        ).astype(F32)
        for part in (out_part, input_part)
    )
    grad_down = apply_mask(contract(act_all, cot_all, 0, 0).astype(BF16), mask_down)
    grad_up = apply_mask(contract(inputs_all, grad_all, 0, 0).astype(BF16), mask_up)
    return (outputs.astype(BF16), grad_inputs.astype(BF16), grad_up, grad_down)


OWN, CORE, X, Y = 0, 1, 2, 4
DIAG = X | Y
SEND = (CORE | DIAG, CORE | X, CORE | Y, CORE)
KEEP = (DIAG, X, Y, OWN)
EARLY = (OWN, CORE, X, Y, CORE | X, CORE | Y)
LATE = (DIAG, CORE | DIAG)
ALL = EARLY + LATE
TABLE = SEND + KEEP + ALL
AT_SEND, AT_KEEP, AT_ALL = 0, len(SEND), len(SEND) + len(KEEP)
AT_LATE = AT_ALL + len(EARLY)


def keep_tiles(dst, weight, keep):
    for k in range(dst.shape[0] // TILE):
        rows = slice(k * TILE, (k + 1) * TILE)
        dst[rows, :] = weight[rows, :] * keep[k : k + 1, :]


def cost(flops, moved):
    return pl.CostEstimate(flops=int(flops), bytes_accessed=int(moved), transcendentals=0)


def params(mib):
    return pltpu.CompilerParams(
        dimension_semantics=("arbitrary",), vmem_limit_bytes=mib * MIB
    )


def weight_specs(weight, keep, share, at, by_rows):
    if by_rows:
        return (
            pl.BlockSpec((share, weight.shape[1]), lambda i, t: (t[at + i], 0)),
            pl.BlockSpec((None,) + keep.shape[1:], lambda i, t: (t[at + i], 0, 0)),
            (share, weight.shape[1]),
        )
    return (
        pl.BlockSpec((weight.shape[0], share), lambda i, t: (0, t[at + i])),
        pl.BlockSpec((keep.shape[0], share), lambda i, t: (0, t[at + i])),
        (weight.shape[0], share),
    )


def whole(array):
    return pl.BlockSpec(array.shape, lambda i, t: (0,) * len(array.shape))


def project(table, parts, weight, keep, share, by_rows, got=None):
    tokens = sum(part.shape[0] for part in parts)
    half = tokens // 2
    wide = parts[0].shape[1]
    at = AT_SEND if got is None else AT_KEEP
    weight_spec, keep_spec, kept_shape = weight_specs(weight, keep, share, at, by_rows)

    def body(table_ref, *refs):
        refs = list(refs)
        part_refs = [refs.pop(0) for _ in parts]
        weight_ref, keep_ref = refs.pop(0), refs.pop(0)
        got_ref = None if got is None else refs.pop(0)
        left, kept = refs[-2:]
        outs = refs[:-2]
        i = pl.program_id(0)

        @pl.when(i == 0)
        def _():
            row = 0
            for ref in part_refs:
                left[row : row + ref.shape[0], :] = ref[...]
                row += ref.shape[0]

        keep_tiles(kept, weight_ref, keep_ref)
        result = contract(left[...], kept[...], 1, 1 if by_rows else 0)
        if got is None:
            outs[0][...] = result.astype(BF16)
            return
        result = (result + got_ref[...].astype(F32)).astype(BF16)
        x_send, y_send, x_keep, y_keep = outs

        @pl.when(i < 2)
        def _():
            x_send[...] = result[:half]

        @pl.when(i >= 2)
        def _():
            x_keep[...] = result[:half]

        @pl.when(i % 2 == 0)
        def _():
            y_send[...] = result[half:]

        @pl.when(i % 2 == 1)
        def _():
            y_keep[...] = result[half:]

    flops = 2 * tokens * wide * share * 4
    moved = 2 * (wide * share * 4 + tokens * share * (4 if got is None else 8) + tokens * wide)
    in_specs = [whole(part) for part in parts] + [weight_spec, keep_spec]
    if got is None:
        out_shape = jax.ShapeDtypeStruct((4, tokens, share), BF16)
        out_specs = pl.BlockSpec((None, tokens, share), lambda i, t: (i, 0, 0))
    else:
        in_specs.append(pl.BlockSpec((None, tokens, share), lambda i, t: (i, 0, 0)))
        out_shape = (jax.ShapeDtypeStruct((2, half, share), BF16),) * 4
        block = (None, half, share)
        out_specs = (
            pl.BlockSpec(block, lambda i, t: (jnp.minimum(i, 1), 0, 0)),
            pl.BlockSpec(block, lambda i, t: (i // 2, 0, 0)),
            pl.BlockSpec(block, lambda i, t: (jnp.maximum(i - 2, 0), 0, 0)),
            pl.BlockSpec(block, lambda i, t: (i // 2, 0, 0)),
        )
    call = pl.pallas_call(
        body,
        out_shape=out_shape,
        grid_spec=pltpu.PrefetchScalarGridSpec(
            num_scalar_prefetch=1,
            grid=(4,),
            in_specs=in_specs,
            out_specs=out_specs,
            scratch_shapes=[
                pltpu.VMEM((tokens, wide), BF16),
                pltpu.VMEM(kept_shape, BF16),
            ],
        ),
        compiler_params=params(40),
        cost_estimate=cost(flops, moved),
    )
    return call(table, *parts, weight, keep, *(() if got is None else (got,)))


def fetch(i, pieces, refs, held, sems):
    copies, n = [], 0
    for at, piece in enumerate(pieces):
        row, own = 0, []
        for array in piece:
            rows = array.shape[0]
            own.append(
                pltpu.make_async_copy(refs[n], held.at[at, pl.ds(row, rows)], sems.at[n])
            )
            row += rows
            n += 1
        copies.append(own)

    @pl.when(i == 0)
    def _():
        for own in copies:
            for copy in own:
                copy.start()

    for at, own in enumerate(copies):

        @pl.when(i == at)
        def _(own=own):
            for copy in own:
                copy.wait()


def gathered(table, pieces, weight, keep, at, by_rows, base=None, blocks=1):
    tokens = sum(array.shape[0] for array in pieces[0])
    share = pieces[0][0].shape[1]
    steps = len(pieces)
    flat = [array for piece in pieces for array in piece]
    wide = weight.shape[1] if by_rows else weight.shape[0]
    weight_spec, keep_spec, kept_shape = weight_specs(weight, keep, share, at, by_rows)
    rows = tokens // blocks

    def body(table_ref, *refs):
        refs = list(refs)
        piece_refs = [refs.pop(0) for _ in flat]
        weight_ref, keep_ref = refs.pop(0), refs.pop(0)
        base_ref = None if base is None else refs.pop(0)
        held, kept, sems = refs[-3:]
        total = refs[-4] if base is not None else refs[0]
        outs = refs[:blocks]
        i = pl.program_id(0)
        fetch(i, pieces, piece_refs, held, sems)
        keep_tiles(kept, weight_ref, keep_ref)
        term = contract(held[i], kept[...], 1, 0 if by_rows else 1)

        @pl.when(i == 0)
        def _():
            total[...] = term if base is None else term + base_ref[...]

        @pl.when(i > 0)
        def _():
            total[...] += term

        if base is not None:

            @pl.when(i == steps - 1)
            def _():
                for k, out in enumerate(outs):
                    out[...] = total[k * rows : (k + 1) * rows, :].astype(BF16)

    in_specs = [pl.BlockSpec(memory_space=pl.ANY)] * len(flat) + [weight_spec, keep_spec]
    scratch = [
        pltpu.VMEM((steps, tokens, share), BF16),
        pltpu.VMEM(kept_shape, BF16),
        pltpu.SemaphoreType.DMA((len(flat),)),
    ]
    args = [*flat, weight, keep]
    if base is None:
        out_shape = jax.ShapeDtypeStruct((tokens, wide), F32)
        out_specs = whole(out_shape)
    else:
        in_specs.append(whole(base))
        args.append(base)
        out_shape = (jax.ShapeDtypeStruct((rows, wide), BF16),) * blocks
        out_specs = (whole(out_shape[0]),) * blocks
        scratch.insert(0, pltpu.VMEM((tokens, wide), F32))
    call = pl.pallas_call(
        body,
        out_shape=out_shape,
        grid_spec=pltpu.PrefetchScalarGridSpec(
            num_scalar_prefetch=1,
            grid=(steps,),
            in_specs=in_specs,
            out_specs=out_specs,
            scratch_shapes=scratch,
        ),
        compiler_params=params(40),
        cost_estimate=cost(
            2 * tokens * share * wide * steps,
            2 * share * (wide + tokens) * steps + 4 * tokens * wide,
        ),
    )
    return call(table, *args)


def weight_gradient(table, pieces, parts, keep, shape, by_rows):
    tokens = sum(part.shape[0] for part in parts)
    share = pieces[0][0].shape[1]
    wide = parts[0].shape[1]
    steps = len(pieces)
    flat = [array for piece in pieces for array in piece]
    weight_spec, keep_spec, _ = weight_specs(
        jax.ShapeDtypeStruct(shape, BF16), keep, share, AT_ALL, by_rows
    )
    span = 2 * TILE

    def body(table_ref, *refs):
        refs = list(refs)
        piece_refs = [refs.pop(0) for _ in flat]
        part_refs = [refs.pop(0) for _ in parts]
        keep_ref, out, held, other, sems = refs
        i = pl.program_id(0)

        @pl.when(i == 0)
        def _():
            row = 0
            for ref in part_refs:
                if by_rows:
                    other[row : row + ref.shape[0], :] = ref[...]
                else:
                    other[:, row : row + ref.shape[0]] = ref[...].T
                row += ref.shape[0]

        fetch(i, pieces, piece_refs, held, sems)
        left = held[i].T if by_rows else other
        right = other[...] if by_rows else held[i]
        for lo in range(0, share if by_rows else wide, span):
            term = contract(left[lo : lo + span, :], right, 1, 0)
            for k in range(0, span, TILE):
                tile = (lo + k) // TILE
                out[lo + k : lo + k + TILE, :] = (
                    term[k : k + TILE].astype(BF16) * keep_ref[tile : tile + 1, :]
                )

    call = pl.pallas_call(
        body,
        out_shape=jax.ShapeDtypeStruct(shape, BF16),
        grid_spec=pltpu.PrefetchScalarGridSpec(
            num_scalar_prefetch=1,
            grid=(steps,),
            in_specs=[pl.BlockSpec(memory_space=pl.ANY)] * len(flat)
            + [whole(part) for part in parts]
            + [keep_spec],
            out_specs=weight_spec,
            scratch_shapes=[
                pltpu.VMEM((steps, tokens, share), BF16),
                pltpu.VMEM((tokens, wide) if by_rows else (wide, tokens), BF16),
                pltpu.SemaphoreType.DMA((len(flat),)),
            ],
        ),
        compiler_params=params(40),
        cost_estimate=cost(
            2 * tokens * share * wide * steps, 2 * share * (wide + tokens) * steps
        ),
    )
    return call(table, *flat, *parts, keep)


def per_device_tuned(n_row, n_col, inputs, w_up, w_down, mask_up, mask_down, cotangent):
    share = w_up.shape[1] // n_row
    table = jnp.asarray(TABLE, jnp.int32) ^ lax.axis_index("row")
    keep_up = jnp.repeat(mask_up.astype(BF16), TILE, axis=1)
    keep_down = jnp.repeat(mask_down.astype(BF16), TILE, axis=1).reshape(
        n_row, share // TILE, w_down.shape[1]
    )

    def across(value, bits):
        return lax.ppermute(value, "row", [(i, i ^ bits) for i in range(n_row)])

    def along(value, shift):
        return lax.ppermute(value, "col", [(i, (i + shift) % n_col) for i in range(n_col)])

    def col_gather(value):
        return [value] + [along(value, k) for k in range(1, n_col)]

    def row_sum(parts, weight, keep, by_rows):
        got = across(project(table, parts, weight, keep, share, by_rows), CORE)
        x_send, y_send, x_keep, y_keep = project(
            table, parts, weight, keep, share, by_rows, got
        )
        x_got, y_got = across(x_send, X), across(y_send, Y)
        x_pass = (x_keep[0].astype(F32) + x_got[0].astype(F32)).astype(BF16)
        y_pass = (y_keep[0].astype(F32) + y_got[0].astype(F32)).astype(BF16)
        x_last, y_last = across(x_pass, Y), across(y_pass, X)
        return jnp.concatenate(
            [
                x_keep[1].astype(F32) + x_got[1].astype(F32) + x_last.astype(F32),
                y_keep[1].astype(F32) + y_got[1].astype(F32) + y_last.astype(F32),
            ]
        )

    def row_gather(value):
        half = value.shape[0] // 2
        from_core, from_x, from_y = (across(value, bits) for bits in (CORE, X, Y))
        core_x, core_y = across(from_x, CORE), across(from_y, CORE)
        diag = (across(from_x[:half], Y), across(from_y[half:], X))
        core_diag = tuple(across(part, CORE) for part in diag)
        early = [(value,), (from_core,), (from_x,), (from_y,), (core_x,), (core_y,)]
        return early, [diag, core_diag]

    def col_sum(blocks):
        terms = [blocks[0]] + [along(blocks[k], -k) for k in range(1, n_col)]
        return functools.reduce(jnp.add, [term.astype(F32) for term in terms]).astype(BF16)

    inputs_all = col_gather(inputs)
    cot_first, *_ = lax.optimization_barrier((cotangent, *inputs_all[1:]))
    cot_all = [cotangent] + [along(cot_first, k) for k in range(1, n_col)]

    hidden = row_sum(inputs_all, w_up, keep_up, False)
    act_early, act_late = row_gather(smooth_gate(hidden).astype(BF16))
    grad_act = row_sum(cot_all, w_down, keep_down, True)
    _, pull = jax.vjp(smooth_gate, hidden)
    grad_early, grad_late = row_gather(pull(grad_act)[0].astype(BF16))

    out_base = gathered(table, act_early, w_down, keep_down, AT_ALL, True)
    outputs = col_sum(
        gathered(table, act_late, w_down, keep_down, AT_LATE, True, out_base, n_col)
    )
    grad_down = weight_gradient(
        table, act_early + act_late, cot_all, keep_down, w_down.shape, True
    )
    in_base = gathered(table, grad_early, w_up, keep_up, AT_ALL, False)
    grad_inputs = col_sum(
        gathered(table, grad_late, w_up, keep_up, AT_LATE, False, in_base, n_col)
    )
    grad_up = weight_gradient(
        table, grad_early + grad_late, inputs_all, keep_up, w_up.shape, False
    )
    return (outputs, grad_inputs, grad_up, grad_down)


def solution(mesh):
    in_specs = (
        P("col", "row"),
        P("row", "col"),
        P("col", "row"),
        P("row", "col"),
        P("col", "row"),
        P("col", "row"),
    )
    out_specs = (P("col", "row"), P("col", "row"), P("row", "col"), P("col", "row"))
    n_row, n_col = mesh.shape["row"], mesh.shape["col"]

    def per_device(inputs, w_up, w_down, mask_up, mask_down, cotangent):
        fits = n_row == 8 and mask_up.shape[1] % n_row == 0
        plan = functools.partial(per_device_tuned, n_row, n_col) if fits else per_device_plain
        return plan(inputs, w_up, w_down, mask_up, mask_down, cotangent)

    return jax.shard_map(
        per_device, mesh=mesh, in_specs=in_specs, out_specs=out_specs, check_vma=False
    )
```

time: 381 us -> 193 us (0.51)
  local copies, waits for them, and re-layouts: 160 us -> 1.66 us
  matrix products: 101 us -> 0 us
  Pallas kernels: 0 us -> 86.2 us
  blocking collectives: 40.1 us -> 0 us
  starting transfers between devices: 0.73 us -> 40.1 us
  between operations: 14.2 us -> 0.96 us
    dot_general x6 -> x0, matrix products: 101 us -> none  [the longest x4 63.8 us: contract(): lax.dot_general(left, right, (((left_dim,), (right_dim,)), ((), ())), pre...]
    unnamed x16 -> x10, local copies, waits for them, and re-layouts: 96.7 us -> 1.01 us
    pallas_call x0 -> x10, Pallas kernels: none -> 86.2 us  [the longest x4 32.4 us: gathered(): return call(table, *args)]
    mul x4 -> x0, local copies, waits for them, and re-layouts: 63.4 us -> none  [apply_mask(): return (shaped * keep).reshape(weight.shape)]
    ppermute x0 -> x40, waiting for transfers between devices: none -> 59.2 us  [the longest x28 33.4 us: across(): return lax.ppermute(value, 'row', [(i, i ^ bits) for i in range(n_row)])]
    reduce_scatter x4 -> x0, waiting for transfers between devices: 58.8 us -> none  [the longest x1 48.9 us: per_device(): lax.psum_scatter(up_part.astype(jnp.bfloat16), 'row', scatter_dimension=0...]
    ppermute x0 -> x40, starting transfers between devices: none -> 40.1 us  [the longest x28 22.1 us: across(): return lax.ppermute(value, 'row', [(i, i ^ bits) for i in range(n_row)])]
    all_gather x2 -> x0, blocking collectives: 40.1 us -> none  [the longest x1 21.8 us: per_device(): lax.all_gather(cotangent, 'col', axis=0, tiled=True)]
  transfers between devices with their start and end apart: 6 -> 40, of which waited for: 2 -> 15; matrix products, arithmetic and copies ran while one was open for 55% -> 2% of each run, Pallas kernels for 0% -> 45%
where the time goes in v1:
time: 193 us; the launch traced here: 192 us
  Pallas kernels  86.2 us (45%)
  waiting for transfers between devices  59.2 us (31%)
  starting transfers between devices  40.1 us (21%)
  other arithmetic  3.96 us (2%)
    ppermute x28, waiting for transfers between devices, across(): return lax.ppermute(value, 'row', [(i, i ^ bits) for i in range(n_row)])  33.4 us
    pallas_call x4, Pallas kernels, gathered(): return call(table, *args)  32.4 us
    pallas_call x4, Pallas kernels, project(): return call(table, *parts, weight, keep, *(() if got is None else (got,)))  27.5 us
    pallas_call x2, Pallas kernels, weight_gradient(): return call(table, *flat, *parts, keep)  26.3 us
    ppermute x12, waiting for transfers between devices, along(): lax.ppermute(value, 'col', [(i, (i + shift) % n_col) for i in range(n_col)])  25.8 us
    ppermute x28, starting transfers between devices, across(): return lax.ppermute(value, 'row', [(i, i ^ bits) for i in range(n_row)])  22.1 us
    ppermute x12, starting transfers between devices, along(): lax.ppermute(value, 'col', [(i, (i + shift) % n_col) for i in range(n_col)])  18.1 us
  transfers between devices with their start and end apart: 40, of which 15 were waited for; matrix products, arithmetic and copies ran while one was open for 2% of the time, Pallas kernels for 45%

profile of v1, /device:TPU:0, one launch (start us, length us, event | category | flops | bytes accessed | tf_op | source)
XLA Modules:
  0.0 192.1 jit_solution(2135971704873681606)
XLA Ops:
  0.6 5.1 %collective-permute-start.2 = (bf16[64,1536]{1,0:T(8,128)(2,1)}, bf16[64,1536]{1,0:T(8,128)(2,1)S(1)}, u32[]{:S(2)}, u32[]{:S(2)}) collective-permute-start(bf16[64,1536]{1,0:T(8,128)(2,1)} %refs_10_.2), channel_id=1, source_target_pairs={{0,3},{1,0},{2,1},{3,2},{4,7},{5,4},{6,5},{7,6},{8,11},{9,8},{10,9... | collective-permute-start | bytes 589832 | tf_op jit(solution)/shard_map/ppermute | solution.py:376
  8.3 3.1 %collective-permute-done.2.refs_3_.refs_13_ = bf16[64,1536]{1,0:T(8,128)(2,1)S(1)} collective-permute-done((bf16[64,1536]{1,0:T(8,128)(2,1)}, bf16[64,1536]{1,0:T(8,128)(2,1)S(1)}, u32[]{:S(2)}, u32[]{:S(2)}) %collective-permute-start.2) | collective-permute-done | bytes 196640 | tf_op jit(solution)/shard_map/ppermute | solution.py:376
  11.4 11.2 %collective-permute-done.1.refs_2_.refs_12_ = bf16[64,1536]{1,0:T(8,128)(2,1)S(1)} collective-permute-done((bf16[64,1536]{1,0:T(8,128)(2,1)}, bf16[64,1536]{1,0:T(8,128)(2,1)S(1)}, u32[]{:S(2)}, u32[]{:S(2)}) %collective-permute-start.1) | collective-permute-done | bytes 196640 | tf_op jit(solution)/shard_map/ppermute | solution.py:376
  23.0 2.4 %collective-permute-start.21 = (bf16[64,1536]{1,0:T(8,128)(2,1)}, bf16[64,1536]{1,0:T(8,128)(2,1)S(1)}, u32[]{:S(2)}, u32[]{:S(2)}) collective-permute-start(bf16[64,1536]{1,0:T(8,128)(2,1)} %refs_10_.3), channel_id=1, source_target_pairs={{0,2},{1,3},{2,0},{3,1},{4,6},{5,7},{6,4},{7,5},{8,10},{9,11},{10,... | collective-permute-start | bytes 589832 | tf_op jit(solution)/shard_map/ppermute | solution.py:376
  28.4 7.4 %shard_map.102 = bf16[4,256,768]{2,1,0:T(8,128)(2,1)} custom-call(s32[16]{0:T(128)S(1)} %broadcast_xor_fusion.table_ref, bf16[64,1536]{1,0:T(8,128)(2,1)S(1)} %copy-done, bf16[64,1536]{1,0:T(8,128)(2,1)S(1)} %collective-permute-done.refs_1_.refs_11_, bf16[64,1536]{1,0:T(8,128)(2,1)S(1)} %collective-permute-done.1.refs_2_.refs_12_, ...), custom_call_target="tpu_custom_call" | custom-call | flops 2415919104 | bytes 11796480 | tf_op jit(solution)/shard_map/pallas_call | solution.py:199
  36.3 6.3 %collective-permute-done.21.refs_2_.refs_12_ = bf16[64,1536]{1,0:T(8,128)(2,1)S(1)} collective-permute-done((bf16[64,1536]{1,0:T(8,128)(2,1)}, bf16[64,1536]{1,0:T(8,128)(2,1)S(1)}, u32[]{:S(2)}, u32[]{:S(2)}) %collective-permute-start.21) | collective-permute-done | bytes 196640 | tf_op jit(solution)/shard_map/ppermute | solution.py:376
  42.6 6.6 %shard_map.106 = bf16[4,256,768]{2,1,0:T(8,128)(2,1)S(1)} custom-call(s32[16]{0:T(128)S(1)} %broadcast_xor_fusion.table_ref, bf16[64,1536]{1,0:T(8,128)(2,1)S(1)} %copy-done.2, bf16[64,1536]{1,0:T(8,128)(2,1)S(1)} %collective-permute-done.20.refs_1_.refs_11_, bf16[64,1536]{1,0:T(8,128)(2,1)S(1)} %collective-permute-done.21.refs_2_.refs_12_, ...), custom_call_target="tpu_custom_call" | custom-call | flops 2415919104 | bytes 11796480 | tf_op jit(solution)/shard_map/pallas_call | solution.py:199
  49.3 6.7 %shard_map.103 = (bf16[2,128,768]{2,1,0:T(8,128)(2,1)S(1)}, bf16[2,128,768]{2,1,0:T(8,128)(2,1)S(1)}, bf16[2,128,768]{2,1,0:T(8,128)(2,1)S(1)}, bf16[2,128,768]{2,1,0:T(8,128)(2,1)S(1)}) custom-call(s32[16]{0:T(128)S(1)} %broadcast_xor_fusion.table_ref, bf16[64,1536]{1,0:T(8,128)(2,1)S(1)} %copy-done.1, ...), custom_call_target="tpu_custom_call" | custom-call | flops 2415919104 | bytes 13369344 | tf_op jit(solution)/shard_map/pallas_call | solution.py:199
  59.1 6.8 %shard_map.107 = (bf16[2,128,768]{2,1,0:T(8,128)(2,1)S(1)}, bf16[2,128,768]{2,1,0:T(8,128)(2,1)S(1)}, bf16[2,128,768]{2,1,0:T(8,128)(2,1)S(1)}, bf16[2,128,768]{2,1,0:T(8,128)(2,1)S(1)}) custom-call(s32[16]{0:T(128)S(1)} %broadcast_xor_fusion.table_ref, bf16[64,1536]{1,0:T(8,128)(2,1)S(1)} %copy-done.2, ...), custom_call_target="tpu_custom_call" | custom-call | flops 2415919104 | bytes 13369344 | tf_op jit(solution)/shard_map/pallas_call | solution.py:199
  71.2 6.7 %collective-permute-done.24 = bf16[2,128,768]{2,1,0:T(8,128)(2,1)S(1)} collective-permute-done((bf16[2,128,768]{2,1,0:T(8,128)(2,1)S(1)}, bf16[2,128,768]{2,1,0:T(8,128)(2,1)S(1)}, u32[]{:S(2)}, u32[]{:S(2)}) %collective-permute-start.24) | collective-permute-done | bytes 393248 | tf_op jit(solution)/shard_map/ppermute | solution.py:373
  80.1 2.6 %collective-permute-done.5 = bf16[128,768]{1,0:T(8,128)(2,1)S(1)} collective-permute-done((bf16[128,768]{1,0:T(8,128)(2,1)S(1)}, bf16[128,768]{1,0:T(8,128)(2,1)S(1)}, u32[]{:S(2)}, u32[]{:S(2)}) %collective-permute-start.5) | collective-permute-done | bytes 196640 | tf_op jit(solution)/shard_map/ppermute | solution.py:373
  82.9 2.8 %collective-permute-done.25 = bf16[128,768]{1,0:T(8,128)(2,1)S(1)} collective-permute-done((bf16[128,768]{1,0:T(8,128)(2,1)S(1)}, bf16[128,768]{1,0:T(8,128)(2,1)S(1)}, u32[]{:S(2)}, u32[]{:S(2)}) %collective-permute-start.25) | collective-permute-done | bytes 196640 | tf_op jit(solution)/shard_map/ppermute | solution.py:373
  90.5 8.0 %collective-permute-done.30.refs_3_ = bf16[256,768]{1,0:T(8,128)(2,1)S(1)} collective-permute-done((bf16[256,768]{1,0:T(8,128)(2,1)S(1)}, bf16[256,768]{1,0:T(8,128)(2,1)S(1)}, u32[]{:S(2)}, u32[]{:S(2)}) %collective-permute-start.30) | collective-permute-done | bytes 393248 | tf_op jit(solution)/shard_map/ppermute | solution.py:373
  100.0 5.1 %collective-permute-done.10.refs_3_ = bf16[256,768]{1,0:T(8,128)(2,1)S(1)} collective-permute-done((bf16[256,768]{1,0:T(8,128)(2,1)S(1)}, bf16[256,768]{1,0:T(8,128)(2,1)S(1)}, u32[]{:S(2)}, u32[]{:S(2)}) %collective-permute-start.10) | collective-permute-done | bytes 393248 | tf_op jit(solution)/shard_map/ppermute | solution.py:373
  105.6 3.1 %collective-permute-done.28.refs_2_ = bf16[256,768]{1,0:T(8,128)(2,1)S(1)} collective-permute-done((bf16[256,768]{1,0:T(8,128)(2,1)S(1)}, bf16[256,768]{1,0:T(8,128)(2,1)S(1)}, u32[]{:S(2)}, u32[]{:S(2)}) %collective-permute-start.28) | collective-permute-done | bytes 393248 | tf_op jit(solution)/shard_map/ppermute | solution.py:373
  111.7 2.9 %collective-permute-start.9 = (bf16[128,768]{1,0:T(8,128)(2,1)S(1)}, bf16[128,768]{1,0:T(8,128)(2,1)S(1)}, u32[]{:S(2)}, u32[]{:S(2)}) collective-permute-start(bf16[128,768]{1,0:T(8,128)(2,1)S(1)} %slice.84), channel_id=1, source_target_pairs={{0,16},{4,20},{8,24},{12,28},{16,0},{20,4},{24,8},{28,12},{1,17},{... | collective-permute-start | bytes 589832 | tf_op jit(solution)/shard_map/ppermute | solution.py:373
  118.8 10.8 %shard_map.104.refs_6_ = f32[256,1536]{1,0:T(8,128)S(1)} custom-call(s32[16]{0:T(128)S(1)} %broadcast_xor_fusion.table_ref, bf16[256,768]{1,0:T(8,128)(2,1)S(1)} %get-tuple-element.39.refs_0_, bf16[256,768]{1,0:T(8,128)(2,1)S(1)} %collective-permute-done.14.refs_1_, bf16[256,768]{1,0:T(8,128)(2,1)S(1)} %collective-permute-done.8.refs_2_, ...), custom_call_target="tpu_custom_call" | custom-call | flops 3623878656 | bytes 18087936 | tf_op jit(solution)/shard_map/pallas_call | solution.py:298
  130.2 5.3 %shard_map.105 = (bf16[64,1536]{1,0:T(8,128)(2,1)S(1)}, bf16[64,1536]{1,0:T(8,128)(2,1)S(1)}, bf16[64,1536]{1,0:T(8,128)(2,1)S(1)}, bf16[64,1536]{1,0:T(8,128)(2,1)S(1)}) custom-call(s32[16]{0:T(128)S(1)} %broadcast_xor_fusion.table_ref, bf16[128,768]{1,0:T(8,128)(2,1)S(1)} %collective-permute-done.9.refs_0_.refs_6_, ...), custom_call_target="tpu_custom_call" | custom-call | flops 1207959552 | bytes 7077888 | tf_op jit(solution)/shard_map/pallas_call | solution.py:298
  137.8 11.0 %shard_map.108.refs_6_ = f32[256,1536]{1,0:T(8,128)S(1)} custom-call(s32[16]{0:T(128)S(1)} %broadcast_xor_fusion.table_ref, bf16[256,768]{1,0:T(8,128)(2,1)S(1)} %get-tuple-element.38.refs_0_, bf16[256,768]{1,0:T(8,128)(2,1)S(1)} %collective-permute-done.34.refs_1_, bf16[256,768]{1,0:T(8,128)(2,1)S(1)} %collective-permute-done.28.refs_2_, ...), custom_call_target="tpu_custom_call" | custom-call | flops 3623878656 | bytes 18087936 | tf_op jit(solution)/shard_map/pallas_call | solution.py:298
  148.8 5.3 %shard_map.109 = (bf16[64,1536]{1,0:T(8,128)(2,1)S(1)}, bf16[64,1536]{1,0:T(8,128)(2,1)S(1)}, bf16[64,1536]{1,0:T(8,128)(2,1)S(1)}, bf16[64,1536]{1,0:T(8,128)(2,1)S(1)}) custom-call(s32[16]{0:T(128)S(1)} %broadcast_xor_fusion.table_ref, bf16[128,768]{1,0:T(8,128)(2,1)S(1)} %collective-permute-done.29.refs_0_.refs_6_, ...), custom_call_target="tpu_custom_call" | custom-call | flops 1207959552 | bytes 7077888 | tf_op jit(solution)/shard_map/pallas_call | solution.py:298
  154.2 2.2 %collective-permute-start.37 = (bf16[64,1536]{1,0:T(8,128)(2,1)S(1)}, bf16[64,1536]{1,0:T(8,128)(2,1)S(1)}, u32[]{:S(2)}, u32[]{:S(2)}) collective-permute-start(bf16[64,1536]{1,0:T(8,128)(2,1)S(1)} %get-tuple-element.35), channel_id=1, source_target_pairs={{0,3},{1,0},{2,1},{3,2},{4,7},{5,4},{6,5},{7,6},{8,11},{9,8},{10,9... | collective-permute-start | bytes 589832 | tf_op jit(solution)/shard_map/ppermute | solution.py:376
  157.0 13.7 %shard_map.110 = bf16[1536,6144]{1,0:T(8,128)(2,1)} custom-call(s32[16]{0:T(128)S(1)} %broadcast_xor_fusion.table_ref, bf16[256,768]{1,0:T(8,128)(2,1)S(1)} %get-tuple-element.38.refs_0_, bf16[256,768]{1,0:T(8,128)(2,1)S(1)} %collective-permute-done.34.refs_1_, bf16[256,768]{1,0:T(8,128)(2,1)S(1)} %collective-permute-done.28.refs_2_, ...), custom_call_target="tpu_custom_call" | custom-call | flops 4831838208 | bytes 22020096 | tf_op jit(solution)/shard_map/pallas_call | solution.py:361
  170.7 12.6 %shard_map.111 = bf16[6144,1536]{1,0:T(8,128)(2,1)} custom-call(s32[16]{0:T(128)S(1)} %broadcast_xor_fusion.table_ref, bf16[256,768]{1,0:T(8,128)(2,1)S(1)} %get-tuple-element.39.refs_0_, bf16[256,768]{1,0:T(8,128)(2,1)S(1)} %collective-permute-done.14.refs_1_, bf16[256,768]{1,0:T(8,128)(2,1)S(1)} %collective-permute-done.8.refs_2_, ...), custom_call_target="tpu_custom_call" | custom-call | flops 4831838208 | bytes 22020096 | tf_op jit(solution)/shard_map/pallas_call | solution.py:361
  186.1 5.2 %collective-permute-done.39 = bf16[64,1536]{1,0:T(8,128)(2,1)S(1)} collective-permute-done((bf16[64,1536]{1,0:T(8,128)(2,1)S(1)}, bf16[64,1536]{1,0:T(8,128)(2,1)S(1)}, u32[]{:S(2)}, u32[]{:S(2)}) %collective-permute-start.39) | collective-permute-done | bytes 196640 | tf_op jit(solution)/shard_map/ppermute | solution.py:376
  (98 shorter events, 38.4 us)
Async XLA Ops:
  5.7 16.9 %collective-permute-start.1 = (bf16[64,1536]{1,0:T(8,128)(2,1)}, bf16[64,1536]{1,0:T(8,128)(2,1)S(1)}, u32[]{:S(2)}, u32[]{:S(2)}) collective-permute-start(bf16[64,1536]{1,0:T(8,128)(2,1)} %refs_10_.2), channel_id=1, source_target_pairs={{0,2},{1,3},{2,0},{3,1},{4,6},{5,7},{6,4},{7,5},{8,10},{9,11},{10,... | collective-permute-start | bytes 589832 | tf_op jit(solution)/shard_map/ppermute | solution.py:376
  5.7 16.9 %collective-permute-start = (bf16[64,1536]{1,0:T(8,128)(2,1)}, bf16[64,1536]{1,0:T(8,128)(2,1)S(1)}, u32[]{:S(2)}, u32[]{:S(2)}) collective-permute-start(bf16[64,1536]{1,0:T(8,128)(2,1)} %refs_10_.2), channel_id=1, source_target_pairs={{0,1},{1,2},{2,3},{3,0},{4,5},{5,6},{6,7},{7,4},{8,9},{9,10},{10,1... | collective-permute-start | bytes 589832 | tf_op jit(solution)/shard_map/ppermute | solution.py:376
  22.6 13.7 %collective-permute-start.22 = (bf16[64,1536]{1,0:T(8,128)(2,1)}, bf16[64,1536]{1,0:T(8,128)(2,1)S(1)}, u32[]{:S(2)}, u32[]{:S(2)}) collective-permute-start(bf16[64,1536]{1,0:T(8,128)(2,1)} %refs_10_.3), channel_id=1, source_target_pairs={{0,3},{1,0},{2,1},{3,2},{4,7},{5,4},{6,5},{7,6},{8,11},{9,8},{10,9... | collective-permute-start | bytes 589832 | tf_op jit(solution)/shard_map/ppermute | solution.py:376
  23.0 19.6 %collective-permute-start.21 = (bf16[64,1536]{1,0:T(8,128)(2,1)}, bf16[64,1536]{1,0:T(8,128)(2,1)S(1)}, u32[]{:S(2)}, u32[]{:S(2)}) collective-permute-start(bf16[64,1536]{1,0:T(8,128)(2,1)} %refs_10_.3), channel_id=1, source_target_pairs={{0,2},{1,3},{2,0},{3,1},{4,6},{5,7},{6,4},{7,5},{8,10},{9,11},{10,... | collective-permute-start | bytes 589832 | tf_op jit(solution)/shard_map/ppermute | solution.py:376
  25.4 17.1 %collective-permute-start.20 = (bf16[64,1536]{1,0:T(8,128)(2,1)}, bf16[64,1536]{1,0:T(8,128)(2,1)S(1)}, u32[]{:S(2)}, u32[]{:S(2)}) collective-permute-start(bf16[64,1536]{1,0:T(8,128)(2,1)} %refs_10_.3), channel_id=1, source_target_pairs={{0,1},{1,2},{2,3},{3,0},{4,5},{5,6},{6,7},{7,4},{8,9},{9,10},{10,1... | collective-permute-start | bytes 589832 | tf_op jit(solution)/shard_map/ppermute | solution.py:376
  35.8 13.5 %collective-permute-start.3 = (bf16[4,256,768]{2,1,0:T(8,128)(2,1)}, bf16[4,256,768]{2,1,0:T(8,128)(2,1)S(1)}, u32[]{:S(2)}, u32[]{:S(2)}) collective-permute-start(bf16[4,256,768]{2,1,0:T(8,128)(2,1)} %shard_map.102), channel_id=1, source_target_pairs={{0,4},{4,0},{8,12},{12,8},{16,20},{20,16},{24,28},{28,24},{1,5},{5... | collective-permute-start | bytes 4718600 | tf_op jit(solution)/shard_map/ppermute | solution.py:373
  67.6 15.1 %collective-permute-start.5 = (bf16[128,768]{1,0:T(8,128)(2,1)S(1)}, bf16[128,768]{1,0:T(8,128)(2,1)S(1)}, u32[]{:S(2)}, u32[]{:S(2)}) collective-permute-start(bf16[128,768]{1,0:T(8,128)(2,1)S(1)} %fusion.7), channel_id=1, source_target_pairs={{0,16},{4,20},{8,24},{12,28},{16,0},{20,4},{24,8},{28,12},{1,17},{... | collective-permute-start | bytes 589832 | tf_op jit(solution)/shard_map/ppermute | solution.py:373
  69.4 13.4 %collective-permute-start.7 = (bf16[128,768]{1,0:T(8,128)(2,1)S(1)}, bf16[128,768]{1,0:T(8,128)(2,1)S(1)}, u32[]{:S(2)}, u32[]{:S(2)}) collective-permute-start(bf16[128,768]{1,0:T(8,128)(2,1)S(1)} %fusion.8), channel_id=1, source_target_pairs={{0,8},{4,12},{8,0},{12,4},{16,24},{20,28},{24,16},{28,20},{1,9},{5... | collective-permute-start | bytes 589832 | tf_op jit(solution)/shard_map/ppermute | solution.py:373
  88.0 17.1 %collective-permute-start.10 = (bf16[256,768]{1,0:T(8,128)(2,1)S(1)}, bf16[256,768]{1,0:T(8,128)(2,1)S(1)}, u32[]{:S(2)}, u32[]{:S(2)}) collective-permute-start(bf16[256,768]{1,0:T(8,128)(2,1)S(1)} %get-tuple-element.39.refs_0_), channel_id=1, source_target_pairs={{0,16},{4,20},{8,24},{12,28},{16,0},{20,4},{24,8},{28,12},{1,17},{... | collective-permute-start | bytes 1179656 | tf_op jit(solution)/shard_map/ppermute | solution.py:373
  88.5 16.6 %collective-permute-start.8 = (bf16[256,768]{1,0:T(8,128)(2,1)S(1)}, bf16[256,768]{1,0:T(8,128)(2,1)S(1)}, u32[]{:S(2)}, u32[]{:S(2)}) collective-permute-start(bf16[256,768]{1,0:T(8,128)(2,1)S(1)} %get-tuple-element.39.refs_0_), channel_id=1, source_target_pairs={{0,8},{4,12},{8,0},{12,4},{16,24},{20,28},{24,16},{28,20},{1,9},{5... | collective-permute-start | bytes 1179656 | tf_op jit(solution)/shard_map/ppermute | solution.py:373
  89.9 18.8 %collective-permute-start.28 = (bf16[256,768]{1,0:T(8,128)(2,1)S(1)}, bf16[256,768]{1,0:T(8,128)(2,1)S(1)}, u32[]{:S(2)}, u32[]{:S(2)}) collective-permute-start(bf16[256,768]{1,0:T(8,128)(2,1)S(1)} %get-tuple-element.38.refs_0_), channel_id=1, source_target_pairs={{0,8},{4,12},{8,0},{12,4},{16,24},{20,28},{24,16},{28,20},{1,9},{5... | collective-permute-start | bytes 1179656 | tf_op jit(solution)/shard_map/ppermute | solution.py:373
  90.5 20.1 %collective-permute-start.14 = (bf16[256,768]{1,0:T(8,128)(2,1)S(1)}, bf16[256,768]{1,0:T(8,128)(2,1)S(1)}, u32[]{:S(2)}, u32[]{:S(2)}) collective-permute-start(bf16[256,768]{1,0:T(8,128)(2,1)S(1)} %get-tuple-element.39.refs_0_), channel_id=1, source_target_pairs={{0,4},{4,0},{8,12},{12,8},{16,20},{20,16},{24,28},{28,24},{1,5},{5... | collective-permute-start | bytes 1179656 | tf_op jit(solution)/shard_map/ppermute | solution.py:373
  105.0 13.2 %collective-permute-start.16 = (bf16[256,768]{1,0:T(8,128)(2,1)S(1)}, bf16[256,768]{1,0:T(8,128)(2,1)S(1)}, u32[]{:S(2)}, u32[]{:S(2)}) collective-permute-start(bf16[256,768]{1,0:T(8,128)(2,1)S(1)} %collective-permute-done.10.refs_3_), channel_id=1, source_target_pairs={{0,4},{4,0},{8,12},{12,8},{16,20},{20,16},{24,28},{28,24},{1,5},{5... | collective-permute-start | bytes 1179656 | tf_op jit(solution)/shard_map/ppermute | solution.py:373
  105.0 13.7 %collective-permute-start.15 = (bf16[256,768]{1,0:T(8,128)(2,1)S(1)}, bf16[256,768]{1,0:T(8,128)(2,1)S(1)}, u32[]{:S(2)}, u32[]{:S(2)}) collective-permute-start(bf16[256,768]{1,0:T(8,128)(2,1)S(1)} %collective-permute-done.8.refs_2_), channel_id=1, source_target_pairs={{0,4},{4,0},{8,12},{12,8},{16,20},{20,16},{24,28},{28,24},{1,5},{5... | collective-permute-start | bytes 1179656 | tf_op jit(solution)/shard_map/ppermute | solution.py:373
  115.4 20.0 %collective-permute-start.34 = (bf16[256,768]{1,0:T(8,128)(2,1)S(1)}, bf16[256,768]{1,0:T(8,128)(2,1)S(1)}, u32[]{:S(2)}, u32[]{:S(2)}) collective-permute-start(bf16[256,768]{1,0:T(8,128)(2,1)S(1)} %get-tuple-element.38.refs_0_), channel_id=1, source_target_pairs={{0,4},{4,0},{8,12},{12,8},{16,20},{20,16},{24,28},{28,24},{1,5},{5... | collective-permute-start | bytes 1179656 | tf_op jit(solution)/shard_map/ppermute | solution.py:373
  116.3 19.2 %collective-permute-start.36 = (bf16[256,768]{1,0:T(8,128)(2,1)S(1)}, bf16[256,768]{1,0:T(8,128)(2,1)S(1)}, u32[]{:S(2)}, u32[]{:S(2)}) collective-permute-start(bf16[256,768]{1,0:T(8,128)(2,1)S(1)} %collective-permute-done.30.refs_3_), channel_id=1, source_target_pairs={{0,4},{4,0},{8,12},{12,8},{16,20},{20,16},{24,28},{28,24},{1,5},{5... | collective-permute-start | bytes 1179656 | tf_op jit(solution)/shard_map/ppermute | solution.py:373
  118.2 17.5 %collective-permute-start.35 = (bf16[256,768]{1,0:T(8,128)(2,1)S(1)}, bf16[256,768]{1,0:T(8,128)(2,1)S(1)}, u32[]{:S(2)}, u32[]{:S(2)}) collective-permute-start(bf16[256,768]{1,0:T(8,128)(2,1)S(1)} %collective-permute-done.28.refs_2_), channel_id=1, source_target_pairs={{0,4},{4,0},{8,12},{12,8},{16,20},{20,16},{24,28},{28,24},{1,5},{5... | collective-permute-start | bytes 1179656 | tf_op jit(solution)/shard_map/ppermute | solution.py:373
  129.6 19.2 %collective-permute-start.33 = (bf16[128,768]{1,0:T(8,128)(2,1)S(1)}, bf16[128,768]{1,0:T(8,128)(2,1)S(1)}, u32[]{:S(2)}, u32[]{:S(2)}) collective-permute-start(bf16[128,768]{1,0:T(8,128)(2,1)S(1)} %collective-permute-done.31.refs_1_.refs_7_), channel_id=1, source_target_pairs={{0,4},{4,0},{8,12},{12,8},{16,20},{20,16},{24,28},{28,24},{1,5},{5... | collective-permute-start | bytes 589832 | tf_op jit(solution)/shard_map/ppermute | solution.py:373
  130.1 18.7 %collective-permute-start.32 = (bf16[128,768]{1,0:T(8,128)(2,1)S(1)}, bf16[128,768]{1,0:T(8,128)(2,1)S(1)}, u32[]{:S(2)}, u32[]{:S(2)}) collective-permute-start(bf16[128,768]{1,0:T(8,128)(2,1)S(1)} %collective-permute-done.29.refs_0_.refs_6_), channel_id=1, source_target_pairs={{0,4},{4,0},{8,12},{12,8},{16,20},{20,16},{24,28},{28,24},{1,5},{5... | collective-permute-start | bytes 589832 | tf_op jit(solution)/shard_map/ppermute | solution.py:373
  135.5 47.9 %collective-permute-start.17 = (bf16[64,1536]{1,0:T(8,128)(2,1)S(1)}, bf16[64,1536]{1,0:T(8,128)(2,1)S(1)}, u32[]{:S(2)}, u32[]{:S(2)}) collective-permute-start(bf16[64,1536]{1,0:T(8,128)(2,1)S(1)} %get-tuple-element.26), channel_id=1, source_target_pairs={{0,3},{1,0},{2,1},{3,2},{4,7},{5,4},{6,5},{7,6},{8,11},{9,8},{10,9... | collective-permute-start | bytes 589832 | tf_op jit(solution)/shard_map/ppermute | solution.py:376
  135.5 49.8 %collective-permute-start.18 = (bf16[64,1536]{1,0:T(8,128)(2,1)S(1)}, bf16[64,1536]{1,0:T(8,128)(2,1)S(1)}, u32[]{:S(2)}, u32[]{:S(2)}) collective-permute-start(bf16[64,1536]{1,0:T(8,128)(2,1)S(1)} %get-tuple-element.27), channel_id=1, source_target_pairs={{0,2},{1,3},{2,0},{3,1},{4,6},{5,7},{6,4},{7,5},{8,10},{9,11},{10,... | collective-permute-start | bytes 589832 | tf_op jit(solution)/shard_map/ppermute | solution.py:376
  135.7 49.7 %collective-permute-start.19 = (bf16[64,1536]{1,0:T(8,128)(2,1)S(1)}, bf16[64,1536]{1,0:T(8,128)(2,1)S(1)}, u32[]{:S(2)}, u32[]{:S(2)}) collective-permute-start(bf16[64,1536]{1,0:T(8,128)(2,1)S(1)} %get-tuple-element.28), channel_id=1, source_target_pairs={{0,1},{1,2},{2,3},{3,0},{4,5},{5,6},{6,7},{7,4},{8,9},{9,10},{10,1... | collective-permute-start | bytes 589832 | tf_op jit(solution)/shard_map/ppermute | solution.py:376
  154.2 32.0 %collective-permute-start.37 = (bf16[64,1536]{1,0:T(8,128)(2,1)S(1)}, bf16[64,1536]{1,0:T(8,128)(2,1)S(1)}, u32[]{:S(2)}, u32[]{:S(2)}) collective-permute-start(bf16[64,1536]{1,0:T(8,128)(2,1)S(1)} %get-tuple-element.35), channel_id=1, source_target_pairs={{0,3},{1,0},{2,1},{3,2},{4,7},{5,4},{6,5},{7,6},{8,11},{9,8},{10,9... | collective-permute-start | bytes 589832 | tf_op jit(solution)/shard_map/ppermute | solution.py:376
  156.3 29.8 %collective-permute-start.38 = (bf16[64,1536]{1,0:T(8,128)(2,1)S(1)}, bf16[64,1536]{1,0:T(8,128)(2,1)S(1)}, u32[]{:S(2)}, u32[]{:S(2)}) collective-permute-start(bf16[64,1536]{1,0:T(8,128)(2,1)S(1)} %get-tuple-element.36), channel_id=1, source_target_pairs={{0,2},{1,3},{2,0},{3,1},{4,6},{5,7},{6,4},{7,5},{8,10},{9,11},{10,... | collective-permute-start | bytes 589832 | tf_op jit(solution)/shard_map/ppermute | solution.py:376
  (20 other events, 193.4 us)

commit v2 on v1

--- a/solution.py
+++ b/solution.py
@@ -83,10 +83,16 @@
 AT_LATE = AT_ALL + len(EARLY)
 
 
-def keep_tiles(dst, weight, keep):
-    for k in range(dst.shape[0] // TILE):
-        rows = slice(k * TILE, (k + 1) * TILE)
-        dst[rows, :] = weight[rows, :] * keep[k : k + 1, :]
+def kept_tiles(weight, keep, columns=slice(None)):
+    strips = range(0, weight.shape[0], TILE)
+    return jnp.concatenate(
+        [weight[lo : lo + TILE, columns] * keep[lo // TILE : lo // TILE + 1, columns] for lo in strips]
+    )
+
+
+def spans(length):
+    span = 2 * TILE if length % (2 * TILE) == 0 else TILE
+    return [slice(lo, lo + span) for lo in range(0, length, span)]
 
 
 def cost(flops, moved):
@@ -104,12 +110,10 @@
         return (
             pl.BlockSpec((share, weight.shape[1]), lambda i, t: (t[at + i], 0)),
             pl.BlockSpec((None,) + keep.shape[1:], lambda i, t: (t[at + i], 0, 0)),
-            (share, weight.shape[1]),
         )
     return (
         pl.BlockSpec((weight.shape[0], share), lambda i, t: (0, t[at + i])),
         pl.BlockSpec((keep.shape[0], share), lambda i, t: (0, t[at + i])),
-        (weight.shape[0], share),
     )
 
 
@@ -122,26 +126,37 @@
     half = tokens // 2
     wide = parts[0].shape[1]
     at = AT_SEND if got is None else AT_KEEP
-    weight_spec, keep_spec, kept_shape = weight_specs(weight, keep, share, at, by_rows)
+    weight_spec, keep_spec = weight_specs(weight, keep, share, at, by_rows)
 
     def body(table_ref, *refs):
         refs = list(refs)
         part_refs = [refs.pop(0) for _ in parts]
         weight_ref, keep_ref = refs.pop(0), refs.pop(0)
         got_ref = None if got is None else refs.pop(0)
-        left, kept = refs[-2:]
-        outs = refs[:-2]
+        held = refs.pop()
+        outs = refs
         i = pl.program_id(0)
 
         @pl.when(i == 0)
         def _():
             row = 0
             for ref in part_refs:
-                left[row : row + ref.shape[0], :] = ref[...]
+                if by_rows:
+                    held[:, row : row + ref.shape[0]] = ref[...].T
+                else:
+                    held[row : row + ref.shape[0], :] = ref[...]
                 row += ref.shape[0]
 
-        keep_tiles(kept, weight_ref, keep_ref)
-        result = contract(left[...], kept[...], 1, 1 if by_rows else 0)
+        if by_rows:
+            result = contract(kept_tiles(weight_ref, keep_ref), held[...], 1, 0).T
+        else:
+            result = jnp.concatenate(
+                [
+                    contract(held[...], kept_tiles(weight_ref, keep_ref, columns), 1, 0)
+                    for columns in spans(share)
+                ],
+                axis=1,
+            )
         if got is None:
             outs[0][...] = result.astype(BF16)
             return
@@ -189,8 +204,7 @@
             in_specs=in_specs,
             out_specs=out_specs,
             scratch_shapes=[
-                pltpu.VMEM((tokens, wide), BF16),
-                pltpu.VMEM(kept_shape, BF16),
+                pltpu.VMEM((wide, tokens) if by_rows else (tokens, wide), BF16),
             ],
         ),
         compiler_params=params(40),
@@ -232,53 +246,62 @@
     steps = len(pieces)
     flat = [array for piece in pieces for array in piece]
     wide = weight.shape[1] if by_rows else weight.shape[0]
-    weight_spec, keep_spec, kept_shape = weight_specs(weight, keep, share, at, by_rows)
+    weight_spec, keep_spec = weight_specs(weight, keep, share, at, by_rows)
     rows = tokens // blocks
+    total_shape = (tokens, wide) if by_rows else (wide, tokens)
 
     def body(table_ref, *refs):
         refs = list(refs)
         piece_refs = [refs.pop(0) for _ in flat]
         weight_ref, keep_ref = refs.pop(0), refs.pop(0)
         base_ref = None if base is None else refs.pop(0)
-        held, kept, sems = refs[-3:]
-        total = refs[-4] if base is not None else refs[0]
+        held, sems = refs[-2:]
+        total = refs[-3] if base is not None else refs[0]
         outs = refs[:blocks]
         i = pl.program_id(0)
         fetch(i, pieces, piece_refs, held, sems)
-        keep_tiles(kept, weight_ref, keep_ref)
-        term = contract(held[i], kept[...], 1, 0 if by_rows else 1)
-
-        @pl.when(i == 0)
-        def _():
-            total[...] = term if base is None else term + base_ref[...]
-
-        @pl.when(i > 0)
-        def _():
-            total[...] += term
+        left = held[i]
+        if not by_rows:
+            left = left.T
+
+        def add(term, columns):
+            @pl.when(i == 0)
+            def _():
+                total[:, columns] = term if base is None else term + base_ref[:, columns]
+
+            @pl.when(i > 0)
+            def _():
+                total[:, columns] += term
+
+        if by_rows:
+            for columns in spans(wide):
+                add(contract(left, kept_tiles(weight_ref, keep_ref, columns), 1, 0), columns)
+        else:
+            add(contract(kept_tiles(weight_ref, keep_ref), left, 1, 0), slice(None))
 
         if base is not None:
 
             @pl.when(i == steps - 1)
             def _():
+                summed = total[...] if by_rows else total[...].T
                 for k, out in enumerate(outs):
-                    out[...] = total[k * rows : (k + 1) * rows, :].astype(BF16)
+                    out[...] = summed[k * rows : (k + 1) * rows, :].astype(BF16)
 
     in_specs = [pl.BlockSpec(memory_space=pl.ANY)] * len(flat) + [weight_spec, keep_spec]
     scratch = [
         pltpu.VMEM((steps, tokens, share), BF16),
-        pltpu.VMEM(kept_shape, BF16),
         pltpu.SemaphoreType.DMA((len(flat),)),
     ]
     args = [*flat, weight, keep]
     if base is None:
-        out_shape = jax.ShapeDtypeStruct((tokens, wide), F32)
+        out_shape = jax.ShapeDtypeStruct(total_shape, F32)
         out_specs = whole(out_shape)
     else:
         in_specs.append(whole(base))
         args.append(base)
         out_shape = (jax.ShapeDtypeStruct((rows, wide), BF16),) * blocks
         out_specs = (whole(out_shape[0]),) * blocks
-        scratch.insert(0, pltpu.VMEM((tokens, wide), F32))
+        scratch.insert(0, pltpu.VMEM(total_shape, F32))
     call = pl.pallas_call(
         body,
         out_shape=out_shape,
@@ -304,10 +327,9 @@
     wide = parts[0].shape[1]
     steps = len(pieces)
     flat = [array for piece in pieces for array in piece]
-    weight_spec, keep_spec, _ = weight_specs(
+    weight_spec, keep_spec = weight_specs(
         jax.ShapeDtypeStruct(shape, BF16), keep, share, AT_ALL, by_rows
     )
-    span = 2 * TILE
 
     def body(table_ref, *refs):
         refs = list(refs)
@@ -327,15 +349,13 @@
                 row += ref.shape[0]
 
         fetch(i, pieces, piece_refs, held, sems)
-        left = held[i].T if by_rows else other
-        right = other[...] if by_rows else held[i]
-        for lo in range(0, share if by_rows else wide, span):
-            term = contract(left[lo : lo + span, :], right, 1, 0)
-            for k in range(0, span, TILE):
-                tile = (lo + k) // TILE
-                out[lo + k : lo + k + TILE, :] = (
-                    term[k : k + TILE].astype(BF16) * keep_ref[tile : tile + 1, :]
-                )
+        left = held[i].T if by_rows else other[...]
+        right = other if by_rows else held.at[i]
+        for columns in spans(out.shape[1]):
+            term = contract(left, right[:, columns], 1, 0).astype(BF16)
+            for k in range(out.shape[0] // TILE):
+                strip = slice(k * TILE, (k + 1) * TILE)
+                out[strip, columns] = term[strip] * keep_ref[k : k + 1, columns]
 
     call = pl.pallas_call(
         body,
@@ -378,7 +398,7 @@
     def col_gather(value):
         return [value] + [along(value, k) for k in range(1, n_col)]
 
-    def row_sum(parts, weight, keep, by_rows):
+    def row_sum(table, parts, weight, keep, by_rows):
         got = across(project(table, parts, weight, keep, share, by_rows), CORE)
         x_send, y_send, x_keep, y_keep = project(
             table, parts, weight, keep, share, by_rows, got
@@ -387,12 +407,13 @@
         x_pass = (x_keep[0].astype(F32) + x_got[0].astype(F32)).astype(BF16)
         y_pass = (y_keep[0].astype(F32) + y_got[0].astype(F32)).astype(BF16)
         x_last, y_last = across(x_pass, Y), across(y_pass, X)
-        return jnp.concatenate(
+        total = jnp.concatenate(
             [
                 x_keep[1].astype(F32) + x_got[1].astype(F32) + x_last.astype(F32),
                 y_keep[1].astype(F32) + y_got[1].astype(F32) + y_last.astype(F32),
             ]
         )
+        return total, x_send
 
     def row_gather(value):
         half = value.shape[0] // 2
@@ -411,9 +432,12 @@
     cot_first, *_ = lax.optimization_barrier((cotangent, *inputs_all[1:]))
     cot_all = [cotangent] + [along(cot_first, k) for k in range(1, n_col)]
 
-    hidden = row_sum(inputs_all, w_up, keep_up, False)
-    act_early, act_late = row_gather(smooth_gate(hidden).astype(BF16))
-    grad_act = row_sum(cot_all, w_down, keep_down, True)
+    hidden, projected = row_sum(table, inputs_all, w_up, keep_up, False)
+    later, _ = lax.optimization_barrier((table, projected))
+    grad_act, back_projected = row_sum(later, cot_all, w_down, keep_down, True)
+    hidden, _ = lax.optimization_barrier((hidden, back_projected))
+    hidden, act = lax.optimization_barrier((hidden, smooth_gate(hidden).astype(BF16)))
+    act_early, act_late = row_gather(act)
     _, pull = jax.vjp(smooth_gate, hidden)
     grad_early, grad_late = row_gather(pull(grad_act)[0].astype(BF16))
 

time: 193 us -> 206 us (1.067)
  Pallas kernels: 86.2 us -> 97.3 us
  waiting for transfers between devices: 59.2 us -> 63.3 us
  starting transfers between devices: 40.1 us -> 38 us
    pallas_call x4, Pallas kernels: 32.4 us -> 41.6 us  [gathered(): return call(table, *args)]
    ppermute x28, waiting for transfers between devices: 33.4 us -> 36.6 us  [across(): return lax.ppermute(value, 'row', [(i, i ^ bits) for i in range(n_row)])]
    ppermute x28, starting transfers between devices: 22.1 us -> 19.9 us  [across(): return lax.ppermute(value, 'row', [(i, i ^ bits) for i in range(n_row)])]
  transfers between devices with their start and end apart: 40 -> 40, of which waited for: 15 -> 16; matrix products, arithmetic and copies ran while one was open for 2% -> 2% of each run, Pallas kernels for 45% -> 34%
where the time goes in v2:
time: 206 us
  Pallas kernels  97.3 us (47%)
  waiting for transfers between devices  63.3 us (31%)
  starting transfers between devices  38 us (18%)
  other arithmetic  4.24 us (2%)
    pallas_call x4, Pallas kernels, gathered(): return call(table, *args)  41.6 us
    ppermute x28, waiting for transfers between devices, across(): return lax.ppermute(value, 'row', [(i, i ^ bits) for i in range(n_row)])  36.6 us
    pallas_call x4, Pallas kernels, project(): return call(table, *parts, weight, keep, *(() if got is None else (got,)))  29.4 us
    ppermute x12, waiting for transfers between devices, along(): lax.ppermute(value, 'col', [(i, (i + shift) % n_col) for i in range(n_col)])  26.7 us
    pallas_call x2, Pallas kernels, weight_gradient(): return call(table, *flat, *parts, keep)  26.3 us
    ppermute x28, starting transfers between devices, across(): return lax.ppermute(value, 'row', [(i, i ^ bits) for i in range(n_row)])  19.9 us
    ppermute x12, starting transfers between devices, along(): lax.ppermute(value, 'col', [(i, (i + shift) % n_col) for i in range(n_col)])  18.1 us
  transfers between devices with their start and end apart: 40, of which 16 were waited for; matrix products, arithmetic and copies ran while one was open for 2% of the time, Pallas kernels for 34%

profile of v2, /device:TPU:0, one launch (start us, length us, event | category | flops | bytes accessed | tf_op | source)
XLA Modules:
  0.0 205.5 jit_solution(14125807919862632114)
XLA Ops:
  0.6 5.1 %collective-permute-start.2 = (bf16[64,1536]{1,0:T(8,128)(2,1)}, bf16[64,1536]{1,0:T(8,128)(2,1)S(1)}, u32[]{:S(2)}, u32[]{:S(2)}) collective-permute-start(bf16[64,1536]{1,0:T(8,128)(2,1)} %refs_10_.2), channel_id=1, source_target_pairs={{0,3},{1,0},{2,1},{3,2},{4,7},{5,4},{6,5},{7,6},{8,11},{9,8},{10,9... | collective-permute-start | bytes 589832 | tf_op jit(solution)/shard_map/ppermute | solution.py:396
  8.3 3.1 %collective-permute-done.2.refs_3_.refs_13_ = bf16[64,1536]{1,0:T(8,128)(2,1)S(1)} collective-permute-done((bf16[64,1536]{1,0:T(8,128)(2,1)}, bf16[64,1536]{1,0:T(8,128)(2,1)S(1)}, u32[]{:S(2)}, u32[]{:S(2)}) %collective-permute-start.2) | collective-permute-done | bytes 196640 | tf_op jit(solution)/shard_map/ppermute | solution.py:396
  11.4 11.2 %collective-permute-done.1.refs_2_.refs_12_ = bf16[64,1536]{1,0:T(8,128)(2,1)S(1)} collective-permute-done((bf16[64,1536]{1,0:T(8,128)(2,1)}, bf16[64,1536]{1,0:T(8,128)(2,1)S(1)}, u32[]{:S(2)}, u32[]{:S(2)}) %collective-permute-start.1) | collective-permute-done | bytes 196640 | tf_op jit(solution)/shard_map/ppermute | solution.py:396
  23.6 7.4 %shard_map.102 = bf16[4,256,768]{2,1,0:T(8,128)(2,1)} custom-call(s32[16]{0:T(128)S(1)} %broadcast_xor_fusion.table_ref, bf16[64,1536]{1,0:T(8,128)(2,1)S(1)} %copy-done.1, bf16[64,1536]{1,0:T(8,128)(2,1)S(1)} %collective-permute-done.refs_1_.refs_11_, bf16[64,1536]{1,0:T(8,128)(2,1)S(1)} %collective-permute-done.1.refs_2_.refs_12_, ...), custom_call_target="tpu_custom_call" | custom-call | flops 2415919104 | bytes 11796480 | tf_op jit(solution)/shard_map/pallas_call | solution.py:213
  31.9 2.5 %collective-permute-start.9 = (bf16[64,1536]{1,0:T(8,128)(2,1)S(1)}, bf16[64,1536]{1,0:T(8,128)(2,1)S(1)}, u32[]{:S(2)}, u32[]{:S(2)}) collective-permute-start(bf16[64,1536]{1,0:T(8,128)(2,1)S(1)} %copy-done), channel_id=1, source_target_pairs={{0,2},{1,3},{2,0},{3,1},{4,6},{5,7},{6,4},{7,5},{8,10},{9,11},{10,... | collective-permute-start | bytes 589832 | tf_op jit(solution)/shard_map/ppermute | solution.py:396
  36.4 6.7 %shard_map.103 = (bf16[2,128,768]{2,1,0:T(8,128)(2,1)S(1)}, bf16[2,128,768]{2,1,0:T(8,128)(2,1)S(1)}, bf16[2,128,768]{2,1,0:T(8,128)(2,1)S(1)}, bf16[2,128,768]{2,1,0:T(8,128)(2,1)S(1)}) custom-call(s32[16]{0:T(128)S(1)} %broadcast_xor_fusion.table_ref, bf16[64,1536]{1,0:T(8,128)(2,1)S(1)} %copy-done.2, ...), custom_call_target="tpu_custom_call" | custom-call | flops 2415919104 | bytes 13369344 | tf_op jit(solution)/shard_map/pallas_call | solution.py:213
  43.1 9.5 %collective-permute-done.9.refs_2_.refs_12_ = bf16[64,1536]{1,0:T(8,128)(2,1)S(1)} collective-permute-done((bf16[64,1536]{1,0:T(8,128)(2,1)S(1)}, bf16[64,1536]{1,0:T(8,128)(2,1)S(1)}, u32[]{:S(2)}, u32[]{:S(2)}) %collective-permute-start.9) | collective-permute-done | bytes 196640 | tf_op jit(solution)/shard_map/ppermute | solution.py:396
  52.6 7.5 %shard_map.104 = bf16[4,256,768]{2,1,0:T(8,128)(2,1)S(1)} custom-call(s32[16]{0:T(128)S(1)} %broadcast_xor_fusion.table_ref, bf16[64,1536]{1,0:T(8,128)(2,1)S(1)} %copy-done, bf16[64,1536]{1,0:T(8,128)(2,1)S(1)} %collective-permute-done.8.refs_1_.refs_11_, bf16[64,1536]{1,0:T(8,128)(2,1)S(1)} %collective-permute-done.9.refs_2_.refs_12_, ...), custom_call_target="tpu_custom_call" | custom-call | flops 2415919104 | bytes 11796480 | tf_op jit(solution)/shard_map/pallas_call | solution.py:213
  63.3 8.5 %collective-permute-done.6 = bf16[2,128,768]{2,1,0:T(8,128)(2,1)S(1)} collective-permute-done((bf16[2,128,768]{2,1,0:T(8,128)(2,1)S(1)}, bf16[2,128,768]{2,1,0:T(8,128)(2,1)S(1)}, u32[]{:S(2)}, u32[]{:S(2)}) %collective-permute-start.6) | collective-permute-done | bytes 393248 | tf_op jit(solution)/shard_map/ppermute | solution.py:393
  75.0 3.3 %collective-permute-done.7 = bf16[128,768]{1,0:T(8,128)(2,1)S(1)} collective-permute-done((bf16[128,768]{1,0:T(8,128)(2,1)S(1)}, bf16[128,768]{1,0:T(8,128)(2,1)S(1)}, u32[]{:S(2)}, u32[]{:S(2)}) %collective-permute-start.7) | collective-permute-done | bytes 196640 | tf_op jit(solution)/shard_map/ppermute | solution.py:393
  79.8 7.7 %shard_map.105 = (bf16[2,128,768]{2,1,0:T(8,128)(2,1)S(1)}, bf16[2,128,768]{2,1,0:T(8,128)(2,1)S(1)}, bf16[2,128,768]{2,1,0:T(8,128)(2,1)S(1)}, bf16[2,128,768]{2,1,0:T(8,128)(2,1)S(1)}) custom-call(s32[16]{0:T(128)S(1)} %broadcast_xor_fusion.table_ref, bf16[64,1536]{1,0:T(8,128)(2,1)S(1)} %copy-done, ...), custom_call_target="tpu_custom_call" | custom-call | flops 2415919104 | bytes 13369344 | tf_op jit(solution)/shard_map/pallas_call | solution.py:213
  91.9 8.0 %collective-permute-done.14.refs_3_ = bf16[256,768]{1,0:T(8,128)(2,1)S(1)} collective-permute-done((bf16[256,768]{1,0:T(8,128)(2,1)S(1)}, bf16[256,768]{1,0:T(8,128)(2,1)S(1)}, u32[]{:S(2)}, u32[]{:S(2)}) %collective-permute-start.14) | collective-permute-done | bytes 393248 | tf_op jit(solution)/shard_map/ppermute | solution.py:393
  102.1 6.2 %collective-permute-done.26 = bf16[2,128,768]{2,1,0:T(8,128)(2,1)S(1)} collective-permute-done((bf16[2,128,768]{2,1,0:T(8,128)(2,1)S(1)}, bf16[2,128,768]{2,1,0:T(8,128)(2,1)S(1)}, u32[]{:S(2)}, u32[]{:S(2)}) %collective-permute-start.26) | collective-permute-done | bytes 393248 | tf_op jit(solution)/shard_map/ppermute | solution.py:393
  110.6 4.8 %collective-permute-done.27 = bf16[128,768]{1,0:T(8,128)(2,1)S(1)} collective-permute-done((bf16[128,768]{1,0:T(8,128)(2,1)S(1)}, bf16[128,768]{1,0:T(8,128)(2,1)S(1)}, u32[]{:S(2)}, u32[]{:S(2)}) %collective-permute-start.27) | collective-permute-done | bytes 196640 | tf_op jit(solution)/shard_map/ppermute | solution.py:393
  119.0 17.1 %shard_map.106.refs_6_ = f32[256,1536]{1,0:T(8,128)S(1)} custom-call(s32[16]{0:T(128)S(1)} %broadcast_xor_fusion.table_ref, bf16[256,768]{1,0:T(8,128)(2,1)S(1)} %fusion.14.refs_0_, bf16[256,768]{1,0:T(8,128)(2,1)S(1)} %collective-permute-done.18.refs_1_, bf16[256,768]{1,0:T(8,128)(2,1)S(1)} %collective-permute-done.12.refs_2_, ...), custom_call_target="tpu_custom_call" | custom-call | flops 3623878656 | bytes 18087936 | tf_op jit(solution)/shard_map/pallas_call | solution.py:321
  136.1 7.9 %shard_map.107 = (bf16[64,1536]{1,0:T(8,128)(2,1)S(1)}, bf16[64,1536]{1,0:T(8,128)(2,1)S(1)}, bf16[64,1536]{1,0:T(8,128)(2,1)S(1)}, bf16[64,1536]{1,0:T(8,128)(2,1)S(1)}) custom-call(s32[16]{0:T(128)S(1)} %broadcast_xor_fusion.table_ref, bf16[128,768]{1,0:T(8,128)(2,1)S(1)} %collective-permute-done.13.refs_0_.refs_6_, ...), custom_call_target="tpu_custom_call" | custom-call | flops 1207959552 | bytes 7077888 | tf_op jit(solution)/shard_map/pallas_call | solution.py:321
  144.4 1.9 collective-permute-start.23
  146.3 12.6 %shard_map.111 = bf16[6144,1536]{1,0:T(8,128)(2,1)} custom-call(s32[16]{0:T(128)S(1)} %broadcast_xor_fusion.table_ref, bf16[256,768]{1,0:T(8,128)(2,1)S(1)} %fusion.14.refs_0_, bf16[256,768]{1,0:T(8,128)(2,1)S(1)} %collective-permute-done.18.refs_1_, bf16[256,768]{1,0:T(8,128)(2,1)S(1)} %collective-permute-done.12.refs_2_, ...), custom_call_target="tpu_custom_call" | custom-call | flops 4831838208 | bytes 22020096 | tf_op jit(solution)/shard_map/pallas_call | solution.py:381
  163.3 3.1 %collective-permute-done.31.refs_1_.refs_7_ = bf16[128,768]{1,0:T(8,128)(2,1)S(1)} collective-permute-done((bf16[128,768]{1,0:T(8,128)(2,1)S(1)}, bf16[128,768]{1,0:T(8,128)(2,1)S(1)}, u32[]{:S(2)}, u32[]{:S(2)}) %collective-permute-start.31) | collective-permute-done | bytes 196640 | tf_op jit(solution)/shard_map/ppermute | solution.py:393
  167.1 11.1 %shard_map.108.refs_6_ = f32[1536,256]{1,0:T(8,128)S(1)} custom-call(s32[16]{0:T(128)S(1)} %broadcast_xor_fusion.table_ref, bf16[256,768]{1,0:T(8,128)(2,1)S(1)} %fusion.6.refs_0_, bf16[256,768]{1,0:T(8,128)(2,1)S(1)} %collective-permute-done.34.refs_1_, bf16[256,768]{1,0:T(8,128)(2,1)S(1)} %collective-permute-done.28.refs_2_, ...), custom_call_target="tpu_custom_call" | custom-call | flops 3623878656 | bytes 18087936 | tf_op jit(solution)/shard_map/pallas_call | solution.py:321
  178.2 5.5 %shard_map.109 = (bf16[64,1536]{1,0:T(8,128)(2,1)S(1)}, bf16[64,1536]{1,0:T(8,128)(2,1)S(1)}, bf16[64,1536]{1,0:T(8,128)(2,1)S(1)}, bf16[64,1536]{1,0:T(8,128)(2,1)S(1)}) custom-call(s32[16]{0:T(128)S(1)} %broadcast_xor_fusion.table_ref, bf16[128,768]{1,0:T(8,128)(2,1)S(1)} %collective-permute-done.29.refs_0_.refs_6_, ...), custom_call_target="tpu_custom_call" | custom-call | flops 1207959552 | bytes 7077888 | tf_op jit(solution)/shard_map/pallas_call | solution.py:321
  183.8 2.2 %collective-permute-start.37 = (bf16[64,1536]{1,0:T(8,128)(2,1)S(1)}, bf16[64,1536]{1,0:T(8,128)(2,1)S(1)}, u32[]{:S(2)}, u32[]{:S(2)}) collective-permute-start(bf16[64,1536]{1,0:T(8,128)(2,1)S(1)} %get-tuple-element.43), channel_id=1, source_target_pairs={{0,3},{1,0},{2,1},{3,2},{4,7},{5,4},{6,5},{7,6},{8,11},{9,8},{10,9... | collective-permute-start | bytes 589832 | tf_op jit(solution)/shard_map/ppermute | solution.py:396
  188.5 13.7 %shard_map.110 = bf16[1536,6144]{1,0:T(8,128)(2,1)} custom-call(s32[16]{0:T(128)S(1)} %broadcast_xor_fusion.table_ref, bf16[256,768]{1,0:T(8,128)(2,1)S(1)} %fusion.6.refs_0_, bf16[256,768]{1,0:T(8,128)(2,1)S(1)} %collective-permute-done.34.refs_1_, bf16[256,768]{1,0:T(8,128)(2,1)S(1)} %collective-permute-done.28.refs_2_, ...), custom_call_target="tpu_custom_call" | custom-call | flops 4831838208 | bytes 22020096 | tf_op jit(solution)/shard_map/pallas_call | solution.py:381
  202.2 2.5 %collective-permute-done.38 = bf16[64,1536]{1,0:T(8,128)(2,1)S(1)} collective-permute-done((bf16[64,1536]{1,0:T(8,128)(2,1)S(1)}, bf16[64,1536]{1,0:T(8,128)(2,1)S(1)}, u32[]{:S(2)}, u32[]{:S(2)}) %collective-permute-start.38) | collective-permute-done | bytes 196640 | tf_op jit(solution)/shard_map/ppermute | solution.py:396
  (100 shorter events, 35.4 us)
Async XLA Ops:
  5.7 16.9 %collective-permute-start.1 = (bf16[64,1536]{1,0:T(8,128)(2,1)}, bf16[64,1536]{1,0:T(8,128)(2,1)S(1)}, u32[]{:S(2)}, u32[]{:S(2)}) collective-permute-start(bf16[64,1536]{1,0:T(8,128)(2,1)} %refs_10_.2), channel_id=1, source_target_pairs={{0,2},{1,3},{2,0},{3,1},{4,6},{5,7},{6,4},{7,5},{8,10},{9,11},{10,... | collective-permute-start | bytes 589832 | tf_op jit(solution)/shard_map/ppermute | solution.py:396
  5.7 16.9 %collective-permute-start = (bf16[64,1536]{1,0:T(8,128)(2,1)}, bf16[64,1536]{1,0:T(8,128)(2,1)S(1)}, u32[]{:S(2)}, u32[]{:S(2)}) collective-permute-start(bf16[64,1536]{1,0:T(8,128)(2,1)} %refs_10_.2), channel_id=1, source_target_pairs={{0,1},{1,2},{2,3},{3,0},{4,5},{5,6},{6,7},{7,4},{8,9},{9,10},{10,1... | collective-permute-start | bytes 589832 | tf_op jit(solution)/shard_map/ppermute | solution.py:396
  31.5 11.6 %collective-permute-start.10 = (bf16[64,1536]{1,0:T(8,128)(2,1)S(1)}, bf16[64,1536]{1,0:T(8,128)(2,1)S(1)}, u32[]{:S(2)}, u32[]{:S(2)}) collective-permute-start(bf16[64,1536]{1,0:T(8,128)(2,1)S(1)} %copy-done), channel_id=1, source_target_pairs={{0,3},{1,0},{2,1},{3,2},{4,7},{5,4},{6,5},{7,6},{8,11},{9,8},{10,9... | collective-permute-start | bytes 589832 | tf_op jit(solution)/shard_map/ppermute | solution.py:396
  31.9 20.6 %collective-permute-start.9 = (bf16[64,1536]{1,0:T(8,128)(2,1)S(1)}, bf16[64,1536]{1,0:T(8,128)(2,1)S(1)}, u32[]{:S(2)}, u32[]{:S(2)}) collective-permute-start(bf16[64,1536]{1,0:T(8,128)(2,1)S(1)} %copy-done), channel_id=1, source_target_pairs={{0,2},{1,3},{2,0},{3,1},{4,6},{5,7},{6,4},{7,5},{8,10},{9,11},{10,... | collective-permute-start | bytes 589832 | tf_op jit(solution)/shard_map/ppermute | solution.py:396
  34.4 18.1 %collective-permute-start.8 = (bf16[64,1536]{1,0:T(8,128)(2,1)S(1)}, bf16[64,1536]{1,0:T(8,128)(2,1)S(1)}, u32[]{:S(2)}, u32[]{:S(2)}) collective-permute-start(bf16[64,1536]{1,0:T(8,128)(2,1)S(1)} %copy-done), channel_id=1, source_target_pairs={{0,1},{1,2},{2,3},{3,0},{4,5},{5,6},{6,7},{7,4},{8,9},{9,10},{10,1... | collective-permute-start | bytes 589832 | tf_op jit(solution)/shard_map/ppermute | solution.py:396
  60.1 19.7 %collective-permute-start.11 = (bf16[4,256,768]{2,1,0:T(8,128)(2,1)S(1)}, bf16[4,256,768]{2,1,0:T(8,128)(2,1)S(1)}, u32[]{:S(2)}, u32[]{:S(2)}) collective-permute-start(bf16[4,256,768]{2,1,0:T(8,128)(2,1)S(1)} %shard_map.104), channel_id=1, source_target_pairs={{0,4},{4,0},{8,12},{12,8},{16,20},{20,16},{24,28},{28,24},{1,5},{5... | collective-permute-start | bytes 4718600 | tf_op jit(solution)/shard_map/ppermute | solution.py:393
  87.8 12.1 %collective-permute-start.14 = (bf16[256,768]{1,0:T(8,128)(2,1)S(1)}, bf16[256,768]{1,0:T(8,128)(2,1)S(1)}, u32[]{:S(2)}, u32[]{:S(2)}) collective-permute-start(bf16[256,768]{1,0:T(8,128)(2,1)S(1)} %fusion.14.refs_0_), channel_id=1, source_target_pairs={{0,16},{4,20},{8,24},{12,28},{16,0},{20,4},{24,8},{28,12},{1,17},{... | collective-permute-start | bytes 1179656 | tf_op jit(solution)/shard_map/ppermute | solution.py:393
  89.3 12.1 %collective-permute-start.12 = (bf16[256,768]{1,0:T(8,128)(2,1)S(1)}, bf16[256,768]{1,0:T(8,128)(2,1)S(1)}, u32[]{:S(2)}, u32[]{:S(2)}) collective-permute-start(bf16[256,768]{1,0:T(8,128)(2,1)S(1)} %fusion.14.refs_0_), channel_id=1, source_target_pairs={{0,8},{4,12},{8,0},{12,4},{16,24},{20,28},{24,16},{28,20},{1,9},{5... | collective-permute-start | bytes 1179656 | tf_op jit(solution)/shard_map/ppermute | solution.py:393
  89.9 18.4 %collective-permute-start.26 = (bf16[2,128,768]{2,1,0:T(8,128)(2,1)S(1)}, bf16[2,128,768]{2,1,0:T(8,128)(2,1)S(1)}, u32[]{:S(2)}, u32[]{:S(2)}) collective-permute-start(bf16[2,128,768]{2,1,0:T(8,128)(2,1)S(1)} %get-tuple-element.40), channel_id=1, source_target_pairs={{0,16},{4,20},{8,24},{12,28},{16,0},{20,4},{24,8},{28,12},{1,17},{... | collective-permute-start | bytes 1179656 | tf_op jit(solution)/shard_map/ppermute | solution.py:393
  90.9 18.9 %collective-permute-start.24 = (bf16[2,128,768]{2,1,0:T(8,128)(2,1)S(1)}, bf16[2,128,768]{2,1,0:T(8,128)(2,1)S(1)}, u32[]{:S(2)}, u32[]{:S(2)}) collective-permute-start(bf16[2,128,768]{2,1,0:T(8,128)(2,1)S(1)} %get-tuple-element.31), channel_id=1, source_target_pairs={{0,8},{4,12},{8,0},{12,4},{16,24},{20,28},{24,16},{28,20},{1,9},{5... | collective-permute-start | bytes 1179656 | tf_op jit(solution)/shard_map/ppermute | solution.py:393
  91.9 24.8 %collective-permute-start.18 = (bf16[256,768]{1,0:T(8,128)(2,1)S(1)}, bf16[256,768]{1,0:T(8,128)(2,1)S(1)}, u32[]{:S(2)}, u32[]{:S(2)}) collective-permute-start(bf16[256,768]{1,0:T(8,128)(2,1)S(1)} %fusion.14.refs_0_), channel_id=1, source_target_pairs={{0,4},{4,0},{8,12},{12,8},{16,20},{20,16},{24,28},{28,24},{1,5},{5... | collective-permute-start | bytes 1179656 | tf_op jit(solution)/shard_map/ppermute | solution.py:393
  99.9 17.4 %collective-permute-start.15 = (bf16[128,768]{1,0:T(8,128)(2,1)S(1)}, bf16[128,768]{1,0:T(8,128)(2,1)S(1)}, u32[]{:S(2)}, u32[]{:S(2)}) collective-permute-start(bf16[128,768]{1,0:T(8,128)(2,1)S(1)} %slice.85), channel_id=1, source_target_pairs={{0,8},{4,12},{8,0},{12,4},{16,24},{20,28},{24,16},{28,20},{1,9},{5... | collective-permute-start | bytes 589832 | tf_op jit(solution)/shard_map/ppermute | solution.py:393
  101.4 17.0 %collective-permute-start.13 = (bf16[128,768]{1,0:T(8,128)(2,1)S(1)}, bf16[128,768]{1,0:T(8,128)(2,1)S(1)}, u32[]{:S(2)}, u32[]{:S(2)}) collective-permute-start(bf16[128,768]{1,0:T(8,128)(2,1)S(1)} %slice.84), channel_id=1, source_target_pairs={{0,16},{4,20},{8,24},{12,28},{16,0},{20,4},{24,8},{28,12},{1,17},{... | collective-permute-start | bytes 589832 | tf_op jit(solution)/shard_map/ppermute | solution.py:393
  116.7 42.3 %collective-permute-start.30 = (bf16[256,768]{1,0:T(8,128)(2,1)S(1)}, bf16[256,768]{1,0:T(8,128)(2,1)S(1)}, u32[]{:S(2)}, u32[]{:S(2)}) collective-permute-start(bf16[256,768]{1,0:T(8,128)(2,1)S(1)} %fusion.6.refs_0_), channel_id=1, source_target_pairs={{0,16},{4,20},{8,24},{12,28},{16,0},{20,4},{24,8},{28,12},{1,17},{... | collective-permute-start | bytes 1179656 | tf_op jit(solution)/shard_map/ppermute | solution.py:393
  117.2 41.8 %collective-permute-start.28 = (bf16[256,768]{1,0:T(8,128)(2,1)S(1)}, bf16[256,768]{1,0:T(8,128)(2,1)S(1)}, u32[]{:S(2)}, u32[]{:S(2)}) collective-permute-start(bf16[256,768]{1,0:T(8,128)(2,1)S(1)} %fusion.6.refs_0_), channel_id=1, source_target_pairs={{0,8},{4,12},{8,0},{12,4},{16,24},{20,28},{24,16},{28,20},{1,9},{5... | collective-permute-start | bytes 1179656 | tf_op jit(solution)/shard_map/ppermute | solution.py:393
  118.5 17.6 %collective-permute-start.17 = (bf16[128,768]{1,0:T(8,128)(2,1)S(1)}, bf16[128,768]{1,0:T(8,128)(2,1)S(1)}, u32[]{:S(2)}, u32[]{:S(2)}) collective-permute-start(bf16[128,768]{1,0:T(8,128)(2,1)S(1)} %collective-permute-done.15.refs_1_.refs_7_), channel_id=1, source_target_pairs={{0,4},{4,0},{8,12},{12,8},{16,20},{20,16},{24,28},{28,24},{1,5},{5... | collective-permute-start | bytes 589832 | tf_op jit(solution)/shard_map/ppermute | solution.py:393
  118.5 17.6 %collective-permute-start.16 = (bf16[128,768]{1,0:T(8,128)(2,1)S(1)}, bf16[128,768]{1,0:T(8,128)(2,1)S(1)}, u32[]{:S(2)}, u32[]{:S(2)}) collective-permute-start(bf16[128,768]{1,0:T(8,128)(2,1)S(1)} %collective-permute-done.13.refs_0_.refs_6_), channel_id=1, source_target_pairs={{0,4},{4,0},{8,12},{12,8},{16,20},{20,16},{24,28},{28,24},{1,5},{5... | collective-permute-start | bytes 589832 | tf_op jit(solution)/shard_map/ppermute | solution.py:393
  144.0 16.0 %collective-permute-start.21 = (bf16[64,1536]{1,0:T(8,128)(2,1)S(1)}, bf16[64,1536]{1,0:T(8,128)(2,1)S(1)}, u32[]{:S(2)}, u32[]{:S(2)}) collective-permute-start(bf16[64,1536]{1,0:T(8,128)(2,1)S(1)} %get-tuple-element.35), channel_id=1, source_target_pairs={{0,3},{1,0},{2,1},{3,2},{4,7},{5,4},{6,5},{7,6},{8,11},{9,8},{10,9... | collective-permute-start | bytes 589832 | tf_op jit(solution)/shard_map/ppermute | solution.py:396
  144.1 18.0 %collective-permute-start.22 = (bf16[64,1536]{1,0:T(8,128)(2,1)S(1)}, bf16[64,1536]{1,0:T(8,128)(2,1)S(1)}, u32[]{:S(2)}, u32[]{:S(2)}) collective-permute-start(bf16[64,1536]{1,0:T(8,128)(2,1)S(1)} %get-tuple-element.36), channel_id=1, source_target_pairs={{0,2},{1,3},{2,0},{3,1},{4,6},{5,7},{6,4},{7,5},{8,10},{9,11},{10,... | collective-permute-start | bytes 589832 | tf_op jit(solution)/shard_map/ppermute | solution.py:396
  144.4 17.7 %collective-permute-start.23 = (bf16[64,1536]{1,0:T(8,128)(2,1)S(1)}, bf16[64,1536]{1,0:T(8,128)(2,1)S(1)}, u32[]{:S(2)}, u32[]{:S(2)}) collective-permute-start(bf16[64,1536]{1,0:T(8,128)(2,1)S(1)} %get-tuple-element.37), channel_id=1, source_target_pairs={{0,1},{1,2},{2,3},{3,0},{4,5},{5,6},{6,7},{7,4},{8,9},{9,10},{10,1... | collective-permute-start | bytes 589832 | tf_op jit(solution)/shard_map/ppermute | solution.py:396
  166.4 11.8 %collective-permute-start.33 = (bf16[128,768]{1,0:T(8,128)(2,1)S(1)}, bf16[128,768]{1,0:T(8,128)(2,1)S(1)}, u32[]{:S(2)}, u32[]{:S(2)}) collective-permute-start(bf16[128,768]{1,0:T(8,128)(2,1)S(1)} %collective-permute-done.31.refs_1_.refs_7_), channel_id=1, source_target_pairs={{0,4},{4,0},{8,12},{12,8},{16,20},{20,16},{24,28},{28,24},{1,5},{5... | collective-permute-start | bytes 589832 | tf_op jit(solution)/shard_map/ppermute | solution.py:393
  183.8 18.4 %collective-permute-start.37 = (bf16[64,1536]{1,0:T(8,128)(2,1)S(1)}, bf16[64,1536]{1,0:T(8,128)(2,1)S(1)}, u32[]{:S(2)}, u32[]{:S(2)}) collective-permute-start(bf16[64,1536]{1,0:T(8,128)(2,1)S(1)} %get-tuple-element.43), channel_id=1, source_target_pairs={{0,3},{1,0},{2,1},{3,2},{4,7},{5,4},{6,5},{7,6},{8,11},{9,8},{10,9... | collective-permute-start | bytes 589832 | tf_op jit(solution)/shard_map/ppermute | solution.py:396
  186.0 18.8 %collective-permute-start.38 = (bf16[64,1536]{1,0:T(8,128)(2,1)S(1)}, bf16[64,1536]{1,0:T(8,128)(2,1)S(1)}, u32[]{:S(2)}, u32[]{:S(2)}) collective-permute-start(bf16[64,1536]{1,0:T(8,128)(2,1)S(1)} %get-tuple-element.44), channel_id=1, source_target_pairs={{0,2},{1,3},{2,0},{3,1},{4,6},{5,7},{6,4},{7,5},{8,10},{9,11},{10,... | collective-permute-start | bytes 589832 | tf_op jit(solution)/shard_map/ppermute | solution.py:396
  186.6 18.1 %collective-permute-start.39 = (bf16[64,1536]{1,0:T(8,128)(2,1)S(1)}, bf16[64,1536]{1,0:T(8,128)(2,1)S(1)}, u32[]{:S(2)}, u32[]{:S(2)}) collective-permute-start(bf16[64,1536]{1,0:T(8,128)(2,1)S(1)} %get-tuple-element.45), channel_id=1, source_target_pairs={{0,1},{1,2},{2,3},{3,0},{4,5},{5,6},{6,7},{7,4},{8,9},{9,10},{10,1... | collective-permute-start | bytes 589832 | tf_op jit(solution)/shard_map/ppermute | solution.py:396
  (20 other events, 144.1 us)
